TPU v7x, 32 devices: a whole 2x2x4 slice. The times are simulated.
32 devices in a mesh: modes: 8 (over y, x, core), sub: 4 (over z).
Axes of the slice: x: 2, y: 2, z: 4, core: 2. Of those that a mesh axis runs over, the one named last changes fastest.
Arguments:
- fields: bfloat16 [2, 384, 1024, 512], P(None, 'sub', 'modes'), may hold values from -6 to 6
- previous: float32 [384, 128, 2, 512], P('sub', 'modes'), may hold values from -6 to 6
- eigen_vectors: float32 [4, 96, 96], P('sub'), may hold values from -0.625 to 0.625
- eigen_map: float32 [4, 96, 96], P('sub'), may hold values from -0.625 to 0.625
- eigen_magnitude: float32 [384], P('sub'), may hold values from 0.5 to 20
- end_rows: float32 [4, 2, 96], P('sub'), may hold values from -0.625 to 0.625
Outputs:
- potential: float32 [384, 128, 2, 512], P('sub', 'modes')
All inputs are finite; a program needn't handle non-finite values.
Results may differ from a plain program's by a relative error of at most 0.0032.
Values may be sent and summed in bfloat16 or wider, within the bound.
No kernel may reach another device: no remote copies, remote signals or barrier semaphores. Data moves between devices by JAX's collectives and lax.ppermute only.
A program may use at most 128 MiB of HBM per device.

v0:
```python
import functools
import math

import jax
import jax.numpy as jnp
import ml_dtypes
import numpy as np
from jax import lax
from jax.experimental import pallas as pl
from jax.experimental.pallas import tpu as pltpu
from jax.sharding import PartitionSpec as P

TWO_PI = 2.0 * math.pi
WAVE_SCALE = 0.0007
SHIFT_TERM = 0.06
CHUNK = 4
GROUP = 2 * CHUNK
LANES = 128
BF16 = jnp.bfloat16
F32 = jnp.float32
VMEM_LIMIT = 57 * 1024 * 1024
TILE = 256
AFTER = 4
SHARES = (3, 1)
JOINED = (False, True)
HEAD_JOINED = True
BODY_BLOCK = 16
HEAD_ROWS = 32


def spanwise_rows(points, modes_count, kz_local):
    grid = np.arange(points)
    waves = np.arange(modes_count * kz_local)
    angle = TWO_PI / points * ((grid[None, :] * waves[:, None]) % points)
    both = np.stack([np.cos(angle), -np.sin(angle)], axis=0) / math.sqrt(points)
    both = both.reshape(2, modes_count, kz_local // CHUNK, CHUNK, points)
    both = both.transpose(1, 2, 0, 3, 4).reshape(modes_count, 2 * kz_local, points)
    return both.astype(np.float32).astype(ml_dtypes.bfloat16)


def streamwise_rows(points, modes_count, count):
    grid = np.arange(points)
    waves = np.arange(count) - count // 2
    angle = TWO_PI / points * ((grid[:, None] * waves[None, :]) % points)
    both = np.concatenate([np.cos(angle), np.sin(angle)], axis=1) / math.sqrt(points)
    both = both.reshape(modes_count, points // modes_count, 2 * count)
    return both.astype(np.float32).astype(ml_dtypes.bfloat16)


def split_pair(value):
    high = value.astype(BF16)
    low = (value - high.astype(F32)).astype(BF16)
    return high, low


def paired_map(matrix):
    high, low = split_pair(matrix)
    return jnp.concatenate(
        [jnp.concatenate([high, high], axis=1), jnp.concatenate([low, low], axis=1)], axis=0
    )


def full_spec():
    return pl.BlockSpec(memory_space=pltpu.VMEM)


def scalar_spec():
    return pl.BlockSpec(memory_space=pltpu.SMEM)


def params(limit=VMEM_LIMIT):
    return pltpu.CompilerParams(vmem_limit_bytes=limit)


def span_kernel(modes_count, sets, block, where, fields, table, *rest):
    outs, rows = rest[:-1], rest[-1]
    per_dest = table.shape[1]
    points = table.shape[2]
    me = where[0]

    @pl.when(pl.program_id(0) == 0)
    def _():
        for step in range(modes_count):
            rows[step * per_dest : (step + 1) * per_dest, :] = table[me ^ step]

    x_local = fields.shape[2]
    for pair in range(block // 2):
        stress = fields[0, 2 * pair : 2 * pair + 2] * fields[1, 2 * pair : 2 * pair + 2]
        stress = stress.reshape(2 * x_local, points)
        spectrum = lax.dot_general(
            rows[...], stress, (((1,), (1,)), ((), ())), preferred_element_type=F32
        )
        span = slice(2 * GROUP * pair, 2 * GROUP * (pair + 1))
        for step in range(modes_count):
            at = 0
            for joined, group in sets:
                for place, chunk in enumerate(group):
                    start = step * per_dest + chunk * GROUP
                    piece = spectrum[start : start + GROUP]
                    piece = jnp.concatenate([piece[:, :x_local], piece[:, x_local:]], axis=0)
                    if joined:
                        outs[at][me ^ step, place, span, :] = piece.astype(BF16)
                    else:
                        outs[at + step][place, span, :] = piece.astype(BF16)
                at += 1 if joined else modes_count


def span_part(fields, table, where, first, count, sets, block):
    modes_count, per_dest, points = table.shape
    x_local = fields.shape[2]
    shapes, specs = [], []
    for joined, group in sets:
        if joined:
            head = (modes_count, len(group))
            shapes.append(jax.ShapeDtypeStruct(head + (count * GROUP, x_local), BF16))
            specs.append(pl.BlockSpec(head + (block * GROUP, x_local), lambda i, w: (0, 0, i, 0)))
            continue
        for _ in range(modes_count):
            shapes.append(jax.ShapeDtypeStruct((len(group), count * GROUP, x_local), BF16))
            specs.append(
                pl.BlockSpec((len(group), block * GROUP, x_local), lambda i, w: (0, i, 0))
            )
    outs = pl.pallas_call(
        functools.partial(span_kernel, modes_count, sets, block),
        out_shape=shapes,
        grid_spec=pltpu.PrefetchScalarGridSpec(
            num_scalar_prefetch=1,
            grid=(count // block,),
            in_specs=[
                pl.BlockSpec((2, block, x_local, points), lambda i, w: (0, first // block + i, 0, 0)),
                pl.BlockSpec(table.shape, lambda i, w: (0, 0, 0)),
            ],
            out_specs=specs,
            scratch_shapes=[pltpu.VMEM((modes_count * per_dest, points), BF16)],
        ),
        compiler_params=params(),
        cost_estimate=pl.CostEstimate(
            flops=2 * count * x_local * points * modes_count * per_dest,
            bytes_accessed=count * x_local * points * 5,
            transcendentals=0,
        ),
        name="span",
    )(where, fields, table)
    result, at = [], 0
    for joined, group in sets:
        if joined:
            result.append(outs[at])
            at += 1
        else:
            result.append(outs[at : at + modes_count])
            at += modes_count
    return result


def kappa_rows(first, rows, count, span):
    waves_x = lax.broadcasted_iota(jnp.int32, (rows, count), 1) - count // 2
    waves_z = lax.broadcasted_iota(jnp.int32, (rows, count), 0) // span + first
    scaled_x = WAVE_SCALE * waves_x.astype(F32)
    scaled_z = WAVE_SCALE * waves_z.astype(F32)
    return SHIFT_TERM + scaled_x * scaled_x + scaled_z * scaled_z


def stream_kernel(modes_count, parts, first, kz_local, where, prev, tables, m_ref, v_ref, e_ref, lam, *rest):
    sources, rest = rest[: sum(n for n, _ in parts)], rest[sum(n for n, _ in parts) :]
    particular, traces_out, forcing = rest
    cheb = m_ref.shape[0]
    count = tables.shape[2] // 2
    points = modes_count * tables.shape[1]
    me = where[0]
    blocks = count // LANES
    place = pl.program_id(0)
    step = pl.program_id(1)

    waves = (lax.broadcasted_iota(jnp.int32, (1, count), 1) - count // 2).astype(F32)
    weight = TWO_PI * waves / points
    row_in = lax.broadcasted_iota(jnp.int32, (GROUP, count), 0)
    signed = jnp.where(row_in < CHUNK, weight, -weight)

    def transform(refs):
        if len(refs) == 1:
            left = [refs[0][d, 0] for d in range(modes_count)]
            origin = list(range(modes_count))
        else:
            left = [ref[0] for ref in refs]
            origin = [me ^ s for s in range(modes_count)]
        left = jnp.concatenate(left, axis=1)
        cosine, sine = [
            jnp.dot(
                left,
                jnp.concatenate([tables[d, :, h * count : (h + 1) * count] for d in origin], axis=0),
                preferred_element_type=F32,
            ).reshape(TILE // GROUP, GROUP, count)
            for h in range(2)
        ]
        cosine = pltpu.roll(cosine, CHUNK, 1)
        total = signed[None] * cosine - weight[None] * sine
        total = total.reshape(TILE, count)
        span = pl.ds(pl.multiple_of(step * TILE, TILE), TILE)
        for b in range(blocks):
            forcing[b, span, :] = total[:, b * LANES : (b + 1) * LANES]

    begin, at = 0, 0
    for arrays, size in parts:
        refs = sources[at : at + arrays]
        pl.when((step >= begin) & (step < begin + size))(functools.partial(transform, refs))
        begin += size
        at += arrays

    @pl.when(step == begin - 1)
    def _():
        map_pair = paired_map(m_ref[...])
        vector_pair = paired_map(v_ref[...])
        end_map = jnp.dot(
            e_ref[...], v_ref[...], preferred_element_type=F32, precision=lax.Precision.HIGHEST
        )
        end_pair = paired_map(end_map)
        magnitude = lam[...]
        width = CHUNK * blocks * 2
        flat = prev.reshape(cheb * width, LANES)
        for k in range(CHUNK):
            sides = []
            for r in range(2):
                for b in range(blocks):
                    new = forcing[b, pl.ds(r * CHUNK + k, cheb, stride=GROUP), :]
                    old = flat[pl.ds((k * blocks + b) * 2 + r, cheb, stride=width), :]
                    sides.append(new + old)
            side = jnp.concatenate(sides, axis=1)
            mapped = jnp.dot(
                map_pair, jnp.concatenate(split_pair(side), axis=0), preferred_element_type=F32
            )
            mapped = mapped[:cheb] + mapped[cheb:]
            kappa_sq = kappa_rows(me * kz_local + (first + place) * CHUNK + k, 1, count, 1)
            inverse = -1.0 / (magnitude + kappa_sq)
            coefficients = mapped * jnp.concatenate([inverse, inverse], axis=1)
            pair = jnp.concatenate(split_pair(coefficients), axis=0)
            value = jnp.dot(vector_pair, pair, preferred_element_type=F32)
            particular[k] = value[:cheb] + value[cheb:]
            ends = jnp.dot(end_pair, pair, preferred_element_type=F32)
            ends = ends[:8] + ends[8:]
            for r in range(2):
                for e in range(2):
                    row = 2 * k + r
                    traces_out[e, row : row + 1, :] = ends[e : e + 1, r * count : (r + 1) * count]


def stream_group(where, prev, tables, m_map, v_map, ends, lam, first, size, sources, offsets, kz_local):
    modes_count = tables.shape[0]
    cheb = m_map.shape[0]
    count = tables.shape[2] // 2
    x_local = tables.shape[1]
    specs, flat, parts, begin = [], [], [], 0
    for source, offset in zip(sources, offsets):
        joined = not isinstance(source, (list, tuple))
        arrays = [source] if joined else list(source)
        held = arrays[0].shape[-2] // TILE

        def index(i, t, w, held=held, offset=offset, begin=begin, head=(0,) * joined):
            return head + (offset + i, jnp.clip(t - begin, 0, held - 1), 0)

        specs += [pl.BlockSpec((modes_count,) * joined + (1, TILE, x_local), index)] * len(arrays)
        flat += arrays
        parts.append((len(arrays), held))
        begin += held
    width = CHUNK * 2 * count // LANES
    flops = 2 * size * begin * TILE * modes_count * x_local * 2 * count

    def whole(array):
        return pl.BlockSpec(array.shape, lambda i, t, w: (0,) * array.ndim)

    return pl.pallas_call(
        functools.partial(stream_kernel, modes_count, parts, first, kz_local),
        out_shape=[
            jax.ShapeDtypeStruct((size * CHUNK, cheb, 2 * count), F32),
            jax.ShapeDtypeStruct((2, size * GROUP, count), F32),
        ],
        grid_spec=pltpu.PrefetchScalarGridSpec(
            num_scalar_prefetch=1,
            grid=(size, begin),
            in_specs=[pl.BlockSpec((cheb, width, LANES), lambda i, t, w: (0, first + i, 0)), full_spec()]
            + [whole(array) for array in (m_map, v_map, ends, lam)]
            + specs,
            out_specs=[
                pl.BlockSpec((CHUNK, cheb, 2 * count), lambda i, t, w: (i, 0, 0)),
                pl.BlockSpec((2, GROUP, count), lambda i, t, w: (0, i, 0)),
            ],
            scratch_shapes=[pltpu.VMEM((count // LANES, begin * TILE, LANES), F32)],
        ),
        compiler_params=params(),
        cost_estimate=pl.CostEstimate(flops=2 * flops, bytes_accessed=4 << 20, transcendentals=0),
        name="stream",
    )(where, prev, tables, m_map, v_map, ends, lam, *flat)


def wall_kernel(kz_local, where, lower_out, upper_out):
    cheb, count = lower_out.shape[1:]
    order = lax.broadcasted_iota(jnp.int32, (cheb, 1), 0).astype(F32)
    points = jnp.cos(math.pi * (order + 1.0) / (cheb + 1))
    chunk = pl.program_id(0)
    for k in range(CHUNK):
        kappa = jnp.sqrt(kappa_rows(where[0] * kz_local + chunk * CHUNK + k, 1, count, 1))
        inverse = 1.0 / (1.0 - jnp.exp(-4.0 * kappa))
        fall = jnp.exp(-kappa * (1.0 + points))
        rise = jnp.exp(-kappa * (1.0 - points))
        lower_out[k] = fall * (1.0 - rise * rise) * inverse
        upper_out[k] = rise * (1.0 - fall * fall) * inverse


def wall_shapes(where, cheb, kz_local, count):
    shape = jax.ShapeDtypeStruct((kz_local, cheb, count), F32)
    return pl.pallas_call(
        functools.partial(wall_kernel, kz_local),
        out_shape=[shape, shape],
        grid=(kz_local // CHUNK,),
        in_specs=[scalar_spec()],
        out_specs=[pl.BlockSpec((CHUNK, cheb, count), lambda i: (i, 0, 0))] * 2,
        compiler_params=params(),
        cost_estimate=pl.CostEstimate(flops=1 << 24, bytes_accessed=6 << 20, transcendentals=2 << 20),
        name="wall",
    )(where)


def finish_kernel(first, kz_local, n_sub, has_old, where, particular, lower, upper, *rest):
    traces = rest[:n_sub]
    out, ordered, solved = rest[n_sub + has_old :]
    cheb = particular.shape[1]
    count = lower.shape[2]
    rows = traces[0].shape[1]
    me = where[1]

    @pl.when(pl.program_id(0) == 0)
    def _():
        for shift in range(n_sub):
            owner = lax.rem(me + n_sub - shift, n_sub)
            ordered[owner] = traces[shift][...]
        kappa = jnp.sqrt(kappa_rows(where[0] * kz_local + first * CHUNK, rows, count, 2))
        decay = jnp.exp(-4.0 * kappa)
        coth_term = (1.0 + decay) / (1.0 - decay)
        csch_term = 2.0 * jnp.exp(-2.0 * kappa) / (1.0 - decay)
        zero = jnp.zeros((rows, count), F32)
        c_prev, d_prev = zero, zero
        factors = []
        for index in range(1, n_sub):
            jump = (ordered[index, 0] - ordered[index - 1, 1]) / kappa
            inverse = 1.0 / (2.0 * coth_term + csch_term * c_prev)
            c_prev = -csch_term * inverse
            d_prev = (jump + csch_term * d_prev) * inverse
            factors.append((c_prev, d_prev))
        solved[0] = zero
        solved[n_sub] = zero
        g_next = zero
        for index in range(n_sub - 1, 0, -1):
            c_value, d_value = factors[index - 1]
            g_next = d_value - c_value * g_next
            solved[index] = g_next

    blocks = count // LANES
    width = CHUNK * 2 * blocks
    flat = out.reshape(cheb * width, LANES)
    chunk = pl.program_id(0)
    for k in range(CHUNK):
        wave = chunk * CHUNK + k
        for r in range(2):
            row = 2 * wave + r
            g_lower = solved[me, pl.ds(row, 1), :]
            g_upper = solved[me + 1, pl.ds(row, 1), :]
            value = (
                particular[k, :, r * count : (r + 1) * count]
                + g_lower * lower[k]
                + g_upper * upper[k]
            )
            for b in range(blocks):
                start = (k * blocks + b) * 2 + r
                flat[pl.ds(start, cheb, stride=width), :] = value[:, b * LANES : (b + 1) * LANES]


def finish_group(where, particular, lower, upper, traces, old, first, kz_local):
    n_sub = len(traces)
    waves, cheb = particular.shape[:2]
    count = lower.shape[2]
    width = CHUNK * 2 * count // LANES
    total = (cheb, kz_local * 2 * count // LANES, LANES)
    has_old = 0 if old is None else 1
    extra = [] if old is None else [old]
    return pl.pallas_call(
        functools.partial(finish_kernel, first, kz_local, n_sub, has_old),
        out_shape=jax.ShapeDtypeStruct(total, F32),
        grid=(waves // CHUNK,),
        in_specs=[
            scalar_spec(),
            pl.BlockSpec((CHUNK, cheb, 2 * count), lambda i: (i, 0, 0)),
            pl.BlockSpec((CHUNK, cheb, count), lambda i: (first + i, 0, 0)),
            pl.BlockSpec((CHUNK, cheb, count), lambda i: (first + i, 0, 0)),
        ]
        + [pl.BlockSpec(traces[0].shape, lambda i: (0, 0, 0))] * n_sub
        + [pl.BlockSpec(memory_space=pl.ANY)] * has_old,
        out_specs=pl.BlockSpec((cheb, width, LANES), lambda i: (0, first + i, 0)),
        scratch_shapes=[
            pltpu.VMEM((n_sub, 2, 2 * waves, count), F32),
            pltpu.VMEM((n_sub + 1, 2 * waves, count), F32),
        ],
        input_output_aliases={4 + n_sub: 0} if has_old else {},
        compiler_params=params(),
        cost_estimate=pl.CostEstimate(flops=1 << 22, bytes_accessed=4 << 20, transcendentals=0),
        name="finish",
    )(where, particular, lower, upper, *traces, *extra)


def step_order(modes_count):
    return sorted(range(1, modes_count), key=lambda step: (-bin(step >> 1).count("1"), step & 1, step))


def chunked(n_sub, modes_count, fields, previous, eigen_vectors, eigen_map, eigen_magnitude, end_rows):
    cheb, x_local, span_points = fields.shape[1:]
    kz_local, count = previous.shape[1], previous.shape[3]
    stream_points = x_local * modes_count
    chunks = kz_local // CHUNK
    where = jnp.stack([lax.axis_index("modes"), lax.axis_index("sub")]).astype(jnp.int32)
    span_table = jnp.asarray(spanwise_rows(span_points, modes_count, kz_local))
    stream_table = jnp.asarray(streamwise_rows(stream_points, modes_count, count))
    ends = jnp.pad(end_rows[0], ((0, 6), (0, 0)))
    lam = eigen_magnitude.reshape(cheb, 1)
    blocks = count // LANES
    prev = previous.reshape(cheb, kz_local, 2, blocks, LANES).transpose(0, 1, 3, 2, 4)
    prev = prev.reshape(cheb, kz_local * blocks * 2, LANES)

    groups, begin = [], 0
    for share in SHARES:
        size = share * chunks // sum(SHARES)
        groups.append(list(range(begin, begin + size)))
        begin += size

    def joined_exchange(value):
        got = lax.all_to_all(value, "modes", 0, 0, tiled=True)
        return got, [got] * modes_count

    def apart_exchange(values):
        got, flying = [None] * modes_count, []
        got[0] = values[0]
        for step in step_order(modes_count):
            pairs = [(d, d ^ step) for d in range(modes_count)]
            got[step] = lax.ppermute(values[step], "modes", pairs)
            flying.append(got[step])
        return got, flying

    everything = list(range(chunks))
    (head,) = span_part(fields, span_table, where, 0, HEAD_ROWS, [(HEAD_JOINED, everything)], 8)
    sets = list(zip(JOINED, groups))
    bodies = span_part(fields, span_table, where, HEAD_ROWS, cheb - HEAD_ROWS, sets, BODY_BLOCK)
    head, before = (joined_exchange if HEAD_JOINED else apart_exchange)(head)
    lower, upper = wall_shapes(where, cheb, kz_local, count)
    arrived = []
    for at, value in enumerate(bodies):
        if at:
            value, lower, upper, _ = lax.optimization_barrier((value, lower, upper, before[AFTER]))
        value, before = (joined_exchange if JOINED[at] else apart_exchange)(value)
        arrived.append(value)

    out = None
    for group, rest in zip(groups, arrived):
        particular, traces = stream_group(
            where, prev, stream_table, eigen_map[0], eigen_vectors[0], ends, lam,
            group[0], len(group), [head, rest], [group[0], 0], kz_local,
        )
        all_traces = [traces] + [
            lax.ppermute(traces, "sub", [(d, (d + shift) % n_sub) for d in range(n_sub)])
            for shift in range(1, n_sub)
        ]
        out = finish_group(where, particular, lower, upper, all_traces, out, group[0], kz_local)
    out = out.reshape(cheb, kz_local, blocks, 2, LANES).transpose(0, 1, 3, 2, 4)
    return out.reshape(cheb, kz_local, 2, count)


def spanwise_table(wave_index, points):
    grid = jnp.arange(points, dtype=jnp.int32)
    phase = grid[:, None] * wave_index[None, :] % points
    angle = TWO_PI / points * phase.astype(jnp.float32)
    scale = 1.0 / math.sqrt(points)
    return (jnp.stack([jnp.cos(angle), -jnp.sin(angle)], axis=1) * scale).astype(jnp.bfloat16)


def streamwise_table(points, count):
    grid = jnp.arange(points, dtype=jnp.int32)
    waves = jnp.arange(count, dtype=jnp.int32) - count // 2
    phase = grid[:, None] * waves[None, :] % points
    angle = TWO_PI / points * phase.astype(jnp.float32)
    cosine = jnp.cos(angle)
    sine = jnp.sin(angle)
    scale = 1.0 / math.sqrt(points)
    real_row = jnp.concatenate([cosine, -sine], axis=1)
    imag_row = jnp.concatenate([sine, cosine], axis=1)
    return (jnp.stack([real_row, imag_row], axis=1) * scale).astype(jnp.bfloat16)


def wall_terms(kappa, cheb):
    points = jnp.cos(math.pi * (jnp.arange(cheb, dtype=jnp.float32) + 1.0) / (cheb + 1))
    points = points[:, None, None, None]
    rate = kappa[None, :, None, :]
    divisor = 1.0 - jnp.exp(-4.0 * rate)
    lower = (
        jnp.exp(-rate * (1.0 + points)) * (1.0 - jnp.exp(-2.0 * rate * (1.0 - points))) / divisor
    )
    upper = (
        jnp.exp(-rate * (1.0 - points)) * (1.0 - jnp.exp(-2.0 * rate * (1.0 + points))) / divisor
    )
    return (lower, upper)


def plain(fields, previous, eigen_vectors, eigen_map, eigen_magnitude, end_rows):
    high = lax.Precision.HIGHEST
    modes_count = lax.axis_size("modes")
    mode_index = lax.axis_index("modes")
    sub_index = lax.axis_index("sub")
    cheb = fields.shape[1]
    x_local = fields.shape[2]
    span_points = fields.shape[3]
    stream_points = x_local * modes_count
    kz_total = span_points // 4
    kz_local = kz_total // modes_count
    kx_count = previous.shape[3]
    stress = (fields[0].astype(jnp.float32) * fields[1].astype(jnp.float32)).astype(jnp.bfloat16)
    wave_index = jnp.arange(kz_total, dtype=jnp.int32)
    table_z = spanwise_table(wave_index, span_points)
    half_spectrum = jnp.einsum(
        "cxz,zrk->cxrk", stress, table_z, preferred_element_type=jnp.float32
    ).astype(jnp.bfloat16)
    table_x = streamwise_table(stream_points, kx_count)
    kept = lax.all_to_all(half_spectrum, "modes", split_axis=3, concat_axis=1, tiled=True)
    stress_hat = jnp.einsum("cxrk,xrq->ckq", kept, table_x, preferred_element_type=jnp.float32)
    stress_hat = stress_hat.reshape(cheb, kz_local, 2, kx_count)
    waves_x = jnp.arange(kx_count, dtype=jnp.float32) - float(kx_count // 2)
    waves_z = (mode_index * kz_local + jnp.arange(kz_local, dtype=jnp.int32)).astype(jnp.float32)
    kappa_sq = (
        SHIFT_TERM + (WAVE_SCALE * waves_x[None, :]) ** 2 + (WAVE_SCALE * waves_z[:, None]) ** 2
    )
    kappa = jnp.sqrt(kappa_sq)
    decay_four = jnp.exp(-4.0 * kappa)
    coth_term = ((1.0 + decay_four) / (1.0 - decay_four))[:, None, :]
    csch_term = (2.0 * jnp.exp(-2.0 * kappa) / (1.0 - decay_four))[:, None, :]
    freq_x = TWO_PI * waves_x / stream_points
    forcing_re = previous[:, :, 0] + freq_x * stress_hat[:, :, 1]
    forcing_im = previous[:, :, 1] - freq_x * stress_hat[:, :, 0]
    forcing = jnp.stack([forcing_re, forcing_im], axis=2)
    coefficients = jnp.einsum("ij,jkrq->ikrq", eigen_map[0], forcing, precision=high)
    coefficients = coefficients / -(
        eigen_magnitude[:, None, None, None] + kappa_sq[None, :, None, :]
    )
    particular = jnp.einsum("ij,jkrq->ikrq", eigen_vectors[0], coefficients, precision=high)
    traces = jnp.einsum("ej,jkrq->ekrq", end_rows[0], particular, precision=high)
    kappa_wide = kappa[:, None, :]
    gathered = lax.all_gather(traces[None], "sub", axis=0, tiled=True)
    jumps = (gathered[1:, 0] - gathered[:-1, 1]) / kappa_wide
    off_term = -csch_term
    diag_term = 2.0 * coth_term

    def forward(carried, jump_value):
        c_prev, d_prev = carried
        divisor = diag_term - off_term * c_prev
        c_next = off_term / divisor
        d_next = (jump_value - off_term * d_prev) / divisor
        return ((c_next, d_next), (c_next, d_next))

    start_state = (
        jnp.zeros((kz_local, 1, kx_count), jnp.float32),
        jnp.zeros((kz_local, 2, kx_count), jnp.float32),
    )
    unused, (c_values, d_values) = lax.scan(forward, start_state, jumps)

    def backward(g_next, factors):
        c_value, d_value = factors
        g_value = d_value - c_value * g_next
        return (g_value, g_value)

    zero_value = jnp.zeros((kz_local, 2, kx_count), jnp.float32)
    unused_last, solved = lax.scan(backward, zero_value, (c_values, d_values), reverse=True)
    padded = jnp.concatenate([zero_value[None], solved, zero_value[None]], axis=0)
    g_lower = lax.dynamic_index_in_dim(padded, sub_index, 0, keepdims=False)
    g_upper = lax.dynamic_index_in_dim(padded, sub_index + 1, 0, keepdims=False)
    lower, upper = wall_terms(kappa, cheb)
    return particular + g_lower[None] * lower + g_upper[None] * upper


def local(n_sub, modes_count, fields, previous, *rest):
    fits = (
        previous.shape[1] % (CHUNK * sum(SHARES)) == 0
        and modes_count & (modes_count - 1) == 0
        and fields.shape[2] == LANES
        and fields.shape[1] % 96 == 0
        and previous.shape[3] % LANES == 0
    )
    if fits:
        return chunked(n_sub, modes_count, fields, previous, *rest)
    return plain(fields, previous, *rest)


def solution(mesh):
    placed = (
        P(None, "sub", "modes", None),
        P("sub", "modes", None, None),
        P("sub", None, None),
        P("sub", None, None),
        P("sub"),
        P("sub", None, None),
    )
    return jax.shard_map(
        functools.partial(local, mesh.shape["sub"], mesh.shape["modes"]),
        mesh=mesh,
        in_specs=placed,
        out_specs=P("sub", "modes", None, None),
        check_vma=False,
    )
```

profile of v0, /device:TPU:0, one launch (start us, length us, event | category | flops | bytes accessed | tf_op | source)
XLA Modules:
  0.0 126.7 jit_solution(10242516280830982360)
XLA Ops:
  0.0 0.6 pad_add_fusion.where
  0.6 6.8 %span.2 = bf16[8,4,256,128]{3,2,1,0:T(8,128)(2,1)} custom-call(s32[2]{0:T(128)} %pad_add_fusion.where, bf16[2,96,128,512]{3,2,1,0:T(8,128)(2,1)} %fields.3, bf16[8,32,512]{2,1,0:T(8,128)(2,1)} %constant.16.clone.table), custom_call_target="tpu_custom_call" | custom-call | flops 1073741824 | bytes 10485760 | tf_op jit(solution)/shard_map/span/pallas_call | solution.py:123
  7.3 5.2 %all-to-all-start = ((bf16[8,4,256,128]{3,2,1,0:T(8,128)(2,1)}), bf16[8,4,256,128]{3,2,1,0:T(8,128)(2,1)S(1)}, u32[]{:S(2)}, u32[]{:S(2)}) async-start(bf16[8,4,256,128]{3,2,1,0:T(8,128)(2,1)} %span.2), calls=%async_computation | async-start | bytes 4194304 | tf_op jit(solution)/shard_map/all_to_all | solution.py:433
  12.5 9.7 %span.3 = (bf16[3,512,128]{2,1,0:T(8,128)(2,1)}, bf16[3,512,128]{2,1,0:T(8,128)(2,1)}, bf16[3,512,128]{2,1,0:T(8,128)(2,1)}, bf16[3,512,128]{2,1,0:T(8,128)(2,1)...) custom-call(s32[2]{0:T(128)} %pad_add_fusion.where, ...), custom_call_target="tpu_custom_call" | custom-call | flops 2147483648 | bytes 20971520 | tf_op jit(solution)/shard_map/span/pallas_call | solution.py:123
  22.2 1.8 %collective-permute-start = (bf16[3,512,128]{2,1,0:T(8,128)(2,1)}, bf16[3,512,128]{2,1,0:T(8,128)(2,1)S(1)}, u32[]{:S(2)}, u32[]{:S(2)}) collective-permute-start(bf16[3,512,128]{2,1,0:T(8,128)(2,1)} %get-tuple-element.26), channel_id=1, source_target_pairs={{0,12},{4,8},{8,4},{12,0},{16,28},{20,24},{24,20},{28,16},{1,13},{... | collective-permute-start | bytes 1179656 | tf_op jit(solution)/shard_map/ppermute | solution.py:441
  24.1 0.4 collective-permute-start.4
  24.4 0.1 collective-permute-start.5
  24.6 1.9 %collective-permute-start.6 = (bf16[3,512,128]{2,1,0:T(8,128)(2,1)}, bf16[3,512,128]{2,1,0:T(8,128)(2,1)}, u32[]{:S(2)}, u32[]{:S(2)}) collective-permute-start(bf16[3,512,128]{2,1,0:T(8,128)(2,1)} %get-tuple-element.35), channel_id=1, source_target_pairs={{0,16},{4,20},{8,24},{12,28},{16,0},{20,4},{24,8},{28,12},{1,17},{... | collective-permute-start | bytes 1179656 | tf_op jit(solution)/shard_map/ppermute | solution.py:441
  26.5 19.8 %collective-permute-done.rest_4_ = bf16[3,512,128]{2,1,0:T(8,128)(2,1)S(1)} collective-permute-done((bf16[3,512,128]{2,1,0:T(8,128)(2,1)}, bf16[3,512,128]{2,1,0:T(8,128)(2,1)S(1)}, u32[]{:S(2)}, u32[]{:S(2)}) %collective-permute-start) | collective-permute-done | bytes 393248 | tf_op jit(solution)/shard_map/ppermute | solution.py:441
  46.2 1.5 %collective-permute-start.8 = (bf16[3,512,128]{2,1,0:T(8,128)(2,1)}, bf16[3,512,128]{2,1,0:T(8,128)(2,1)}, u32[]{:S(2)}, u32[]{:S(2)}) collective-permute-start(bf16[3,512,128]{2,1,0:T(8,128)(2,1)} %get-tuple-element.37), channel_id=1, source_target_pairs={{0,24},{4,28},{8,16},{12,20},{16,8},{20,12},{24,0},{28,4},{1,25},{... | collective-permute-start | bytes 1179656 | tf_op jit(solution)/shard_map/ppermute | solution.py:441
  47.8 1.9 %collective-permute-start.9 = (bf16[3,512,128]{2,1,0:T(8,128)(2,1)}, bf16[3,512,128]{2,1,0:T(8,128)(2,1)}, u32[]{:S(2)}, u32[]{:S(2)}) collective-permute-start(bf16[3,512,128]{2,1,0:T(8,128)(2,1)} %get-tuple-element.38), channel_id=1, source_target_pairs={{0,28},{4,24},{8,20},{12,16},{16,12},{20,8},{24,4},{28,0},{1,29},{... | collective-permute-start | bytes 1179656 | tf_op jit(solution)/shard_map/ppermute | solution.py:441
  49.7 4.8 %wall.1 = (f32[16,96,512]{2,1,0:T(8,128)}, f32[16,96,512]{2,1,0:T(8,128)}) custom-call(s32[2]{0:T(128)} %pad_add_fusion.where), custom_call_target="tpu_custom_call" | custom-call | flops 16777216 | bytes 6291456 | tf_op jit(solution)/shard_map/wall/pallas_call | solution.py:310
  54.5 3.6 %all-to-all-start.1 = ((bf16[8,1,512,128]{3,2,1,0:T(8,128)(2,1)}), bf16[8,1,512,128]{3,2,1,0:T(8,128)(2,1)S(1)}, u32[]{:S(2)}, u32[]{:S(2)}) async-start(bf16[8,1,512,128]{3,2,1,0:T(8,128)(2,1)} %get-tuple-element.27), calls=%async_computation.1 | async-start | bytes 2097152 | tf_op jit(solution)/shard_map/all_to_all | solution.py:433
  58.0 0.7 copy.11.lam
  58.8 0.6 pad.4.e_ref
  59.4 5.8 %collective-permute-done.8.rest_7_ = bf16[3,512,128]{2,1,0:T(8,128)(2,1)} collective-permute-done((bf16[3,512,128]{2,1,0:T(8,128)(2,1)}, bf16[3,512,128]{2,1,0:T(8,128)(2,1)}, u32[]{:S(2)}, u32[]{:S(2)}) %collective-permute-start.8) | collective-permute-done | bytes 393248 | tf_op jit(solution)/shard_map/ppermute | solution.py:441
  65.2 7.5 %collective-permute-done.9.rest_8_ = bf16[3,512,128]{2,1,0:T(8,128)(2,1)} collective-permute-done((bf16[3,512,128]{2,1,0:T(8,128)(2,1)}, bf16[3,512,128]{2,1,0:T(8,128)(2,1)}, u32[]{:S(2)}, u32[]{:S(2)}) %collective-permute-start.9) | collective-permute-done | bytes 393248 | tf_op jit(solution)/shard_map/ppermute | solution.py:441
  72.6 20.2 %stream.3 = (f32[12,96,1024]{2,1,0:T(8,128)}, f32[2,24,512]{2,1,0:T(8,128)}) custom-call(s32[2]{0:T(128)} %pad_add_fusion.where, f32[96,128,128]{2,1,0:T(8,128)} %bitcast.18, bf16[8,128,1024]{2,1,0:T(8,128)(2,1)} %constant.17.clone.tables, f32[96,96]{1,0:T(8,128)} %bitcast.20, f32[96,96]{1,0:T(8,128)} %bitcast.22, f32[8,96]{1,0:T(8,128)} %pad.4.e_ref, ...), custom_call_target="tpu_custom_call" | custom-call | flops 9663676416 | bytes 4194304 | tf_op jit(solution)/shard_map/stream/pallas_call | solution.py:270
  92.8 3.6 %collective-permute-start.12 = (f32[2,24,512]{2,1,0:T(8,128)}, f32[2,24,512]{2,1,0:T(8,128)S(1)}, u32[]{:S(2)}, u32[]{:S(2)}) collective-permute-start(f32[2,24,512]{2,1,0:T(8,128)} %get-tuple-element.40.rest_0_), channel_id=1, source_target_pairs={{0,3},{1,0},{2,1},{3,2},{4,7},{5,4},{6,5},{7,6},{8,11},{9,8},{10,9... | collective-permute-start | bytes 294920 | tf_op jit(solution)/shard_map/ppermute | solution.py:465
  96.5 1.0 collective-permute-start.10
  97.5 1.0 copy-done.1
  98.5 9.3 %stream.2 = (f32[4,96,1024]{2,1,0:T(8,128)}, f32[2,8,512]{2,1,0:T(8,128)}) custom-call(s32[2]{0:T(128)} %pad_add_fusion.where, f32[96,128,128]{2,1,0:T(8,128)} %bitcast.19, bf16[8,128,1024]{2,1,0:T(8,128)(2,1)} %constant.17.clone.tables, f32[96,96]{1,0:T(8,128)} %bitcast.21, f32[96,96]{1,0:T(8,128)} %bitcast.23, f32[8,96]{1,0:T(8,128)} %pad.4.e_ref, ...), custom_call_target="tpu_custom_call" | custom-call | flops 3221225472 | bytes 4194304 | tf_op jit(solution)/shard_map/stream/pallas_call | solution.py:270
  107.8 2.8 %collective-permute-start.3 = (f32[2,8,512]{2,1,0:T(8,128)}, f32[2,8,512]{2,1,0:T(8,128)S(1)}, u32[]{:S(2)}, u32[]{:S(2)}) collective-permute-start(f32[2,8,512]{2,1,0:T(8,128)} %get-tuple-element.31.rest_0_), channel_id=1, source_target_pairs={{0,3},{1,0},{2,1},{3,2},{4,7},{5,4},{6,5},{7,6},{8,11},{9,8},{10,9... | collective-permute-start | bytes 98312 | tf_op jit(solution)/shard_map/ppermute | solution.py:465
  110.6 1.1 collective-permute-start.2
  111.8 0.6 copy-done.2
  112.4 0.1 copy-done.3
  112.4 0.0 copy-done.4
  112.4 9.2 %finish.2.rest_4_ = f32[96,128,128]{2,1,0:T(8,128)} custom-call(s32[2]{0:T(128)} %pad_add_fusion.where, f32[12,96,1024]{2,1,0:T(8,128)} %get-tuple-element.39.particular, f32[16,96,512]{2,1,0:T(8,128)} %get-tuple-element.29.lower, f32[16,96,512]{2,1,0:T(8,128)} %get-tuple-element.30.upper, f32[2,24,512]{2,1,0:T(8,128)} %get-tuple-element.40.rest_0_, ...), custom_call_target="tpu_custom_call" | custom-call | flops 4194304 | bytes 4194304 | tf_op jit(solution)/shard_map/finish/pallas_call | solution.py:384
  121.7 0.6 copy-done.5
  122.3 0.0 copy-done.6
  122.3 0.0 copy-done.7
  122.3 4.3 %finish.3 = f32[96,128,128]{2,1,0:T(8,128)} custom-call(s32[2]{0:T(128)} %pad_add_fusion.where, f32[4,96,1024]{2,1,0:T(8,128)} %get-tuple-element.28.particular, f32[16,96,512]{2,1,0:T(8,128)} %get-tuple-element.29.lower, f32[16,96,512]{2,1,0:T(8,128)} %get-tuple-element.30.upper, ...), custom_call_target="tpu_custom_call", output_to_operand_aliasing={{}: (8, {})} | custom-call | flops 4194304 | bytes 4194304 | tf_op jit(solution)/shard_map/finish/pallas_call | solution.py:384
  (32 shorter events, 0.1 us)
Async XLA Ops:
  7.3 47.1 %all-to-all-start = ((bf16[8,4,256,128]{3,2,1,0:T(8,128)(2,1)}), bf16[8,4,256,128]{3,2,1,0:T(8,128)(2,1)S(1)}, u32[]{:S(2)}, u32[]{:S(2)}) async-start(bf16[8,4,256,128]{3,2,1,0:T(8,128)(2,1)} %span.2), calls=%async_computation | async-start | bytes 4194304 | tf_op jit(solution)/shard_map/all_to_all | solution.py:433
  22.2 35.8 %copy-start.9 = (f32[96]{0:T(128)S(1)}, f32[96]{0:T(128)}, u32[]{:S(2)}) copy-start(f32[96]{0:T(128)} %param.12) | copy-start | bytes 1156
  22.2 36.5 %copy-start.8 = (f32[1,2,96]{2,1,0:T(2,128)S(1)}, f32[1,2,96]{2,1,0:T(2,128)}, u32[]{:S(2)}) copy-start(f32[1,2,96]{2,1,0:T(2,128)} %param.13) | copy-start | bytes 2308
  22.2 24.0 %collective-permute-start = (bf16[3,512,128]{2,1,0:T(8,128)(2,1)}, bf16[3,512,128]{2,1,0:T(8,128)(2,1)S(1)}, u32[]{:S(2)}, u32[]{:S(2)}) collective-permute-start(bf16[3,512,128]{2,1,0:T(8,128)(2,1)} %get-tuple-element.26), channel_id=1, source_target_pairs={{0,12},{4,8},{8,4},{12,0},{16,28},{20,24},{24,20},{28,16},{1,13},{... | collective-permute-start | bytes 1179656 | tf_op jit(solution)/shard_map/ppermute | solution.py:441
  24.1 23.7 %collective-permute-start.4 = (bf16[3,512,128]{2,1,0:T(8,128)(2,1)}, bf16[3,512,128]{2,1,0:T(8,128)(2,1)S(1)}, u32[]{:S(2)}, u32[]{:S(2)}) collective-permute-start(bf16[3,512,128]{2,1,0:T(8,128)(2,1)} %get-tuple-element.33), channel_id=1, source_target_pairs={{0,4},{4,0},{8,12},{12,8},{16,20},{20,16},{24,28},{28,24},{1,5},{5... | collective-permute-start | bytes 1179656 | tf_op jit(solution)/shard_map/ppermute | solution.py:441
  24.4 34.9 %collective-permute-start.5 = (bf16[3,512,128]{2,1,0:T(8,128)(2,1)}, bf16[3,512,128]{2,1,0:T(8,128)(2,1)}, u32[]{:S(2)}, u32[]{:S(2)}) collective-permute-start(bf16[3,512,128]{2,1,0:T(8,128)(2,1)} %get-tuple-element.34), channel_id=1, source_target_pairs={{0,8},{4,12},{8,0},{12,4},{16,24},{20,28},{24,16},{28,20},{1,9},{5... | collective-permute-start | bytes 1179656 | tf_op jit(solution)/shard_map/ppermute | solution.py:441
  24.6 34.8 %collective-permute-start.6 = (bf16[3,512,128]{2,1,0:T(8,128)(2,1)}, bf16[3,512,128]{2,1,0:T(8,128)(2,1)}, u32[]{:S(2)}, u32[]{:S(2)}) collective-permute-start(bf16[3,512,128]{2,1,0:T(8,128)(2,1)} %get-tuple-element.35), channel_id=1, source_target_pairs={{0,16},{4,20},{8,24},{12,28},{16,0},{20,4},{24,8},{28,12},{1,17},{... | collective-permute-start | bytes 1179656 | tf_op jit(solution)/shard_map/ppermute | solution.py:441
  26.5 32.9 %collective-permute-start.7 = (bf16[3,512,128]{2,1,0:T(8,128)(2,1)}, bf16[3,512,128]{2,1,0:T(8,128)(2,1)}, u32[]{:S(2)}, u32[]{:S(2)}) collective-permute-start(bf16[3,512,128]{2,1,0:T(8,128)(2,1)} %get-tuple-element.36), channel_id=1, source_target_pairs={{0,20},{4,16},{8,28},{12,24},{16,4},{20,0},{24,12},{28,8},{1,21},{... | collective-permute-start | bytes 1179656 | tf_op jit(solution)/shard_map/ppermute | solution.py:441
  46.2 26.4 %copy-start.10 = (bf16[3,512,128]{2,1,0:T(8,128)(2,1)}, bf16[3,512,128]{2,1,0:T(8,128)(2,1)S(1)}, u32[]{:S(2)}) copy-start(bf16[3,512,128]{2,1,0:T(8,128)(2,1)S(1)} %collective-permute-done.rest_4_) | copy-start | bytes 1179652
  46.2 18.9 %collective-permute-start.8 = (bf16[3,512,128]{2,1,0:T(8,128)(2,1)}, bf16[3,512,128]{2,1,0:T(8,128)(2,1)}, u32[]{:S(2)}, u32[]{:S(2)}) collective-permute-start(bf16[3,512,128]{2,1,0:T(8,128)(2,1)} %get-tuple-element.37), channel_id=1, source_target_pairs={{0,24},{4,28},{8,16},{12,20},{16,8},{20,12},{24,0},{28,4},{1,25},{... | collective-permute-start | bytes 1179656 | tf_op jit(solution)/shard_map/ppermute | solution.py:441
  47.8 6.7 %copy-start.11 = (bf16[3,512,128]{2,1,0:T(8,128)(2,1)}, bf16[3,512,128]{2,1,0:T(8,128)(2,1)S(1)}, u32[]{:S(2)}) copy-start(bf16[3,512,128]{2,1,0:T(8,128)(2,1)S(1)} %collective-permute-done.4.rest_2_) | copy-start | bytes 1179652
  47.8 24.9 %collective-permute-start.9 = (bf16[3,512,128]{2,1,0:T(8,128)(2,1)}, bf16[3,512,128]{2,1,0:T(8,128)(2,1)}, u32[]{:S(2)}, u32[]{:S(2)}) collective-permute-start(bf16[3,512,128]{2,1,0:T(8,128)(2,1)} %get-tuple-element.38), channel_id=1, source_target_pairs={{0,28},{4,24},{8,20},{12,16},{16,12},{20,8},{24,4},{28,0},{1,29},{... | collective-permute-start | bytes 1179656 | tf_op jit(solution)/shard_map/ppermute | solution.py:441
  54.5 18.2 %copy-start = (bf16[8,4,256,128]{3,2,1,0:T(8,128)(2,1)}, bf16[8,4,256,128]{3,2,1,0:T(8,128)(2,1)S(1)}, u32[]{:S(2)}) copy-start(bf16[8,4,256,128]{3,2,1,0:T(8,128)(2,1)S(1)} %all-to-all-done.rest_0_) | copy-start | bytes 6291460
  54.5 43.0 %all-to-all-start.1 = ((bf16[8,1,512,128]{3,2,1,0:T(8,128)(2,1)}), bf16[8,1,512,128]{3,2,1,0:T(8,128)(2,1)S(1)}, u32[]{:S(2)}, u32[]{:S(2)}) async-start(bf16[8,1,512,128]{3,2,1,0:T(8,128)(2,1)} %get-tuple-element.27), calls=%async_computation.1 | async-start | bytes 2097152 | tf_op jit(solution)/shard_map/all_to_all | solution.py:433
  92.8 18.9 %collective-permute-start.12 = (f32[2,24,512]{2,1,0:T(8,128)}, f32[2,24,512]{2,1,0:T(8,128)S(1)}, u32[]{:S(2)}, u32[]{:S(2)}) collective-permute-start(f32[2,24,512]{2,1,0:T(8,128)} %get-tuple-element.40.rest_0_), channel_id=1, source_target_pairs={{0,3},{1,0},{2,1},{3,2},{4,7},{5,4},{6,5},{7,6},{8,11},{9,8},{10,9... | collective-permute-start | bytes 294920 | tf_op jit(solution)/shard_map/ppermute | solution.py:465
  96.5 15.2 %collective-permute-start.11 = (f32[2,24,512]{2,1,0:T(8,128)}, f32[2,24,512]{2,1,0:T(8,128)S(1)}, u32[]{:S(2)}, u32[]{:S(2)}) collective-permute-start(f32[2,24,512]{2,1,0:T(8,128)} %get-tuple-element.40.rest_0_), channel_id=1, source_target_pairs={{0,2},{1,3},{2,0},{3,1},{4,6},{5,7},{6,4},{7,5},{8,10},{9,11},{10,... | collective-permute-start | bytes 294920 | tf_op jit(solution)/shard_map/ppermute | solution.py:465
  96.5 15.3 %collective-permute-start.10 = (f32[2,24,512]{2,1,0:T(8,128)}, f32[2,24,512]{2,1,0:T(8,128)S(1)}, u32[]{:S(2)}, u32[]{:S(2)}) collective-permute-start(f32[2,24,512]{2,1,0:T(8,128)} %get-tuple-element.40.rest_0_), channel_id=1, source_target_pairs={{0,1},{1,2},{2,3},{3,0},{4,5},{5,6},{6,7},{7,4},{8,9},{9,10},{10,1... | collective-permute-start | bytes 294920 | tf_op jit(solution)/shard_map/ppermute | solution.py:465
  97.5 1.0 copy-start.1
  107.8 13.9 %collective-permute-start.3 = (f32[2,8,512]{2,1,0:T(8,128)}, f32[2,8,512]{2,1,0:T(8,128)S(1)}, u32[]{:S(2)}, u32[]{:S(2)}) collective-permute-start(f32[2,8,512]{2,1,0:T(8,128)} %get-tuple-element.31.rest_0_), channel_id=1, source_target_pairs={{0,3},{1,0},{2,1},{3,2},{4,7},{5,4},{6,5},{7,6},{8,11},{9,8},{10,9... | collective-permute-start | bytes 98312 | tf_op jit(solution)/shard_map/ppermute | solution.py:465
  110.6 11.1 %collective-permute-start.2 = (f32[2,8,512]{2,1,0:T(8,128)}, f32[2,8,512]{2,1,0:T(8,128)S(1)}, u32[]{:S(2)}, u32[]{:S(2)}) collective-permute-start(f32[2,8,512]{2,1,0:T(8,128)} %get-tuple-element.31.rest_0_), channel_id=1, source_target_pairs={{0,2},{1,3},{2,0},{3,1},{4,6},{5,7},{6,4},{7,5},{8,10},{9,11},{10,... | collective-permute-start | bytes 98312 | tf_op jit(solution)/shard_map/ppermute | solution.py:465
  111.7 0.6 copy-start.2
  111.7 10.0 %collective-permute-start.1 = (f32[2,8,512]{2,1,0:T(8,128)}, f32[2,8,512]{2,1,0:T(8,128)S(1)}, u32[]{:S(2)}, u32[]{:S(2)}) collective-permute-start(f32[2,8,512]{2,1,0:T(8,128)} %get-tuple-element.31.rest_0_), channel_id=1, source_target_pairs={{0,1},{1,2},{2,3},{3,0},{4,5},{5,6},{6,7},{7,4},{8,9},{9,10},{10,1... | collective-permute-start | bytes 98312 | tf_op jit(solution)/shard_map/ppermute | solution.py:465
  111.7 0.7 copy-start.3
  111.8 0.7 copy-start.4
  121.7 0.6 copy-start.5
  121.7 0.6 copy-start.6
  121.7 0.6 copy-start.7
where the time goes:
time: 127 us
  Pallas kernels  64.3 us (51%)
  waiting for transfers between devices  33.1 us (26%)
  starting transfers between devices  25 us (20%)
  local copies, waits for them, and re-layouts  3.61 us (3%)
    ppermute x7, waiting for transfers between devices, apart_exchange(): got[step] = lax.ppermute(values[step], 'modes', pairs)  33 us
    pallas_call x2, Pallas kernels, stream_group(): pl.pallas_call(functools.partial(stream_kernel, modes_count, parts, first...  29.5 us
    pallas_call x2, Pallas kernels, span_part(): pl.pallas_call(functools.partial(span_kernel, modes_count, sets, block),...  16.5 us
    pallas_call x2, Pallas kernels, finish_group(): pl.pallas_call(functools.partial(finish_kernel, first, kz_local, n_sub, h...  13.6 us
    all_to_all x2, starting transfers between devices, joined_exchange(): got = lax.all_to_all(value, 'modes', 0, 0, tiled=True)  8.74 us
    ppermute x6, starting transfers between devices, chunked(): lax.ppermute(traces, 'sub', [(d, (d + shift) % n_sub) for d in range(n_su...  8.59 us
    ppermute x7, starting transfers between devices, apart_exchange(): got[step] = lax.ppermute(values[step], 'modes', pairs)  7.65 us
    pallas_call x1, Pallas kernels, wall_shapes(): pl.pallas_call(functools.partial(wall_kernel, kz_local), out_shape=[shape...  4.78 us
  transfers between devices with their start and end apart: 15, of which 3 were waited for; matrix products, arithmetic and copies ran while one was open for 1% of the time, Pallas kernels for 42%

commit v1 on v0

--- a/solution.py
+++ b/solution.py
@@ -18,14 +18,16 @@
 LANES = 128
 BF16 = jnp.bfloat16
 F32 = jnp.float32
-VMEM_LIMIT = 57 * 1024 * 1024
+VMEM_LIMIT = 50 * 1024 * 1024
 TILE = 256
-AFTER = 4
-SHARES = (3, 1)
+Y_PARTS = 1
+AFTER = 6
+SHARES = (2, 2)
 JOINED = (False, True)
 HEAD_JOINED = True
 BODY_BLOCK = 16
 HEAD_ROWS = 32
+HEAD_BLOCK = 16
 
 
 def spanwise_rows(points, modes_count, kz_local):
@@ -160,64 +162,95 @@
     return SHIFT_TERM + scaled_x * scaled_x + scaled_z * scaled_z
 
 
-def stream_kernel(modes_count, parts, first, kz_local, where, prev, tables, m_ref, v_ref, e_ref, lam, *rest):
-    sources, rest = rest[: sum(n for n, _ in parts)], rest[sum(n for n, _ in parts) :]
-    particular, traces_out, forcing = rest
+def stream_kernel(modes_count, parts, first, size, kz_local, where, prev, table_ref, m_ref, v_ref, e_ref, lam, *rest):
+    arrays_in = sum(part[0] for part in parts)
+    sources, rest = rest[:arrays_in], rest[arrays_in:]
+    particular, traces_out, held, old_rows, tables, done, forcing, sems, own_sems, out_sems = rest
     cheb = m_ref.shape[0]
+    x_local = tables.shape[1]
     count = tables.shape[2] // 2
-    points = modes_count * tables.shape[1]
+    width = old_rows.shape[2]
+    points = modes_count * x_local
     me = where[0]
     blocks = count // LANES
-    place = pl.program_id(0)
-    step = pl.program_id(1)
+
+    def copies(place):
+        result, at, row = [], 0, 0
+        for part, (arrays, offset, rows) in enumerate(parts):
+            for d in range(modes_count):
+                if arrays == 1:
+                    source = sources[at].at[d, offset + place]
+                else:
+                    source = sources[at + d].at[offset + place]
+                target = held.at[place, d, pl.ds(row, rows)]
+                result.append(pltpu.make_async_copy(source, target, sems.at[place, part, d]))
+            at += arrays
+            row += rows
+        return result
+
+    def old_copy(place):
+        source = prev.at[:, pl.ds((first + place) * width, width)]
+        return pltpu.make_async_copy(source, old_rows.at[place], own_sems.at[place])
+
+    def done_copy(wave):
+        return pltpu.make_async_copy(done.at[wave], particular.at[wave], out_sems.at[wave])
+
+    table_copy = pltpu.make_async_copy(table_ref, tables, own_sems.at[size])
+    table_copy.start()
+    for place in range(size):
+        for copy in copies(place):
+            copy.start()
+        old_copy(place).start()
 
     waves = (lax.broadcasted_iota(jnp.int32, (1, count), 1) - count // 2).astype(F32)
     weight = TWO_PI * waves / points
     row_in = lax.broadcasted_iota(jnp.int32, (GROUP, count), 0)
     signed = jnp.where(row_in < CHUNK, weight, -weight)
-
-    def transform(refs):
-        if len(refs) == 1:
-            left = [refs[0][d, 0] for d in range(modes_count)]
-            origin = list(range(modes_count))
-        else:
-            left = [ref[0] for ref in refs]
-            origin = [me ^ s for s in range(modes_count)]
-        left = jnp.concatenate(left, axis=1)
-        cosine, sine = [
-            jnp.dot(
-                left,
-                jnp.concatenate([tables[d, :, h * count : (h + 1) * count] for d in origin], axis=0),
-                preferred_element_type=F32,
-            ).reshape(TILE // GROUP, GROUP, count)
-            for h in range(2)
-        ]
-        cosine = pltpu.roll(cosine, CHUNK, 1)
-        total = signed[None] * cosine - weight[None] * sine
-        total = total.reshape(TILE, count)
-        span = pl.ds(pl.multiple_of(step * TILE, TILE), TILE)
-        for b in range(blocks):
-            forcing[b, span, :] = total[:, b * LANES : (b + 1) * LANES]
-
-    begin, at = 0, 0
-    for arrays, size in parts:
-        refs = sources[at : at + arrays]
-        pl.when((step >= begin) & (step < begin + size))(functools.partial(transform, refs))
-        begin += size
-        at += arrays
-
-    @pl.when(step == begin - 1)
-    def _():
-        map_pair = paired_map(m_ref[...])
-        vector_pair = paired_map(v_ref[...])
-        end_map = jnp.dot(
-            e_ref[...], v_ref[...], preferred_element_type=F32, precision=lax.Precision.HIGHEST
-        )
-        end_pair = paired_map(end_map)
-        magnitude = lam[...]
-        width = CHUNK * blocks * 2
-        flat = prev.reshape(cheb * width, LANES)
+    map_pair = paired_map(m_ref[...])
+    end_map = jnp.dot(
+        e_ref[...], v_ref[...], preferred_element_type=F32, precision=lax.Precision.HIGHEST
+    )
+    vector_pair = paired_map(jnp.concatenate([v_ref[...], end_map], axis=0))
+    magnitude = lam[...]
+    extended = cheb + end_map.shape[0]
+
+    for place in range(size):
+        for copy in copies(place):
+            copy.wait()
+        if place == 0:
+            table_copy.wait()
+        row = 0
+        for arrays, _, rows in parts:
+            origin = [d if arrays == 1 else me ^ d for d in range(modes_count)]
+            base = row
+
+            def transform(step, unused):
+                span = pl.ds(pl.multiple_of(base + step * TILE, TILE), TILE)
+                left = jnp.concatenate([held[place, d, span, :] for d in range(modes_count)], axis=1)
+                cosine, sine = [
+                    jnp.dot(
+                        left,
+                        jnp.concatenate(
+                            [tables[d, :, h * count : (h + 1) * count] for d in origin], axis=0
+                        ),
+                        preferred_element_type=F32,
+                    ).reshape(TILE // GROUP, GROUP, count)
+                    for h in range(2)
+                ]
+                cosine = pltpu.roll(cosine, CHUNK, 1)
+                total = signed[None] * cosine - weight[None] * sine
+                total = total.reshape(TILE, count)
+                for b in range(blocks):
+                    forcing[b, span, :] = total[:, b * LANES : (b + 1) * LANES]
+                return unused
+
+            lax.fori_loop(0, rows // TILE, transform, 0)
+            row += rows
+
+        old_copy(place).wait()
+        flat = old_rows.at[place].reshape(cheb * width, LANES)
         for k in range(CHUNK):
+            wave = (first + place) * CHUNK + k
             sides = []
             for r in range(2):
                 for b in range(blocks):
@@ -229,18 +262,22 @@
                 map_pair, jnp.concatenate(split_pair(side), axis=0), preferred_element_type=F32
             )
             mapped = mapped[:cheb] + mapped[cheb:]
-            kappa_sq = kappa_rows(me * kz_local + (first + place) * CHUNK + k, 1, count, 1)
+            kappa_sq = kappa_rows(me * kz_local + wave, 1, count, 1)
             inverse = -1.0 / (magnitude + kappa_sq)
             coefficients = mapped * jnp.concatenate([inverse, inverse], axis=1)
             pair = jnp.concatenate(split_pair(coefficients), axis=0)
             value = jnp.dot(vector_pair, pair, preferred_element_type=F32)
-            particular[k] = value[:cheb] + value[cheb:]
-            ends = jnp.dot(end_pair, pair, preferred_element_type=F32)
-            ends = ends[:8] + ends[8:]
+            value = value[:extended] + value[extended:]
+            done[place * CHUNK + k] = value[:cheb]
+            done_copy(place * CHUNK + k).start()
             for r in range(2):
                 for e in range(2):
-                    row = 2 * k + r
-                    traces_out[e, row : row + 1, :] = ends[e : e + 1, r * count : (r + 1) * count]
+                    row = 2 * (place * CHUNK + k) + r
+                    traces_out[e, row : row + 1, :] = value[
+                        cheb + e : cheb + e + 1, r * count : (r + 1) * count
+                    ]
+    for wave in range(size * CHUNK):
+        done_copy(wave).wait()
 
 
 def stream_group(where, prev, tables, m_map, v_map, ends, lam, first, size, sources, offsets, kz_local):
@@ -248,43 +285,34 @@
     cheb = m_map.shape[0]
     count = tables.shape[2] // 2
     x_local = tables.shape[1]
-    specs, flat, parts, begin = [], [], [], 0
+    flat, parts = [], []
     for source, offset in zip(sources, offsets):
-        joined = not isinstance(source, (list, tuple))
-        arrays = [source] if joined else list(source)
-        held = arrays[0].shape[-2] // TILE
-
-        def index(i, t, w, held=held, offset=offset, begin=begin, head=(0,) * joined):
-            return head + (offset + i, jnp.clip(t - begin, 0, held - 1), 0)
-
-        specs += [pl.BlockSpec((modes_count,) * joined + (1, TILE, x_local), index)] * len(arrays)
+        arrays = list(source) if isinstance(source, (list, tuple)) else [source]
+        parts.append((len(arrays), offset, arrays[0].shape[-2]))
         flat += arrays
-        parts.append((len(arrays), held))
-        begin += held
-    width = CHUNK * 2 * count // LANES
-    flops = 2 * size * begin * TILE * modes_count * x_local * 2 * count
-
-    def whole(array):
-        return pl.BlockSpec(array.shape, lambda i, t, w: (0,) * array.ndim)
-
+    rows = sum(part[2] for part in parts)
+    flops = 2 * size * rows * modes_count * x_local * 2 * count
     return pl.pallas_call(
-        functools.partial(stream_kernel, modes_count, parts, first, kz_local),
+        functools.partial(stream_kernel, modes_count, parts, first, size, kz_local),
         out_shape=[
             jax.ShapeDtypeStruct((size * CHUNK, cheb, 2 * count), F32),
             jax.ShapeDtypeStruct((2, size * GROUP, count), F32),
         ],
-        grid_spec=pltpu.PrefetchScalarGridSpec(
-            num_scalar_prefetch=1,
-            grid=(size, begin),
-            in_specs=[pl.BlockSpec((cheb, width, LANES), lambda i, t, w: (0, first + i, 0)), full_spec()]
-            + [whole(array) for array in (m_map, v_map, ends, lam)]
-            + specs,
-            out_specs=[
-                pl.BlockSpec((CHUNK, cheb, 2 * count), lambda i, t, w: (i, 0, 0)),
-                pl.BlockSpec((2, GROUP, count), lambda i, t, w: (0, i, 0)),
-            ],
-            scratch_shapes=[pltpu.VMEM((count // LANES, begin * TILE, LANES), F32)],
-        ),
+        in_specs=[scalar_spec()]
+        + [pl.BlockSpec(memory_space=pl.ANY)] * 2
+        + [full_spec()] * 4
+        + [pl.BlockSpec(memory_space=pl.ANY)] * len(flat),
+        out_specs=[pl.BlockSpec(memory_space=pl.ANY), full_spec()],
+        scratch_shapes=[
+            pltpu.VMEM((size, modes_count, rows, x_local), BF16),
+            pltpu.VMEM((size, cheb, CHUNK * 2 * count // LANES, LANES), F32),
+            pltpu.VMEM(tables.shape, BF16),
+            pltpu.VMEM((size * CHUNK, cheb, 2 * count), F32),
+            pltpu.VMEM((count // LANES, rows, LANES), F32),
+            pltpu.SemaphoreType.DMA((size, len(parts), modes_count)),
+            pltpu.SemaphoreType.DMA((size + 1,)),
+            pltpu.SemaphoreType.DMA((size * CHUNK,)),
+        ],
         compiler_params=params(),
         cost_estimate=pl.CostEstimate(flops=2 * flops, bytes_accessed=4 << 20, transcendentals=0),
         name="stream",
@@ -322,12 +350,12 @@
 def finish_kernel(first, kz_local, n_sub, has_old, where, particular, lower, upper, *rest):
     traces = rest[:n_sub]
     out, ordered, solved = rest[n_sub + has_old :]
-    cheb = particular.shape[1]
+    held = particular.shape[1]
     count = lower.shape[2]
     rows = traces[0].shape[1]
     me = where[1]
 
-    @pl.when(pl.program_id(0) == 0)
+    @pl.when((pl.program_id(0) == 0) & (pl.program_id(1) == 0))
     def _():
         for shift in range(n_sub):
             owner = lax.rem(me + n_sub - shift, n_sub)
@@ -355,7 +383,7 @@
 
     blocks = count // LANES
     width = CHUNK * 2 * blocks
-    flat = out.reshape(cheb * width, LANES)
+    flat = out.reshape(held * width, LANES)
     chunk = pl.program_id(0)
     for k in range(CHUNK):
         wave = chunk * CHUNK + k
@@ -370,7 +398,7 @@
             )
             for b in range(blocks):
                 start = (k * blocks + b) * 2 + r
-                flat[pl.ds(start, cheb, stride=width), :] = value[:, b * LANES : (b + 1) * LANES]
+                flat[pl.ds(start, held, stride=width), :] = value[:, b * LANES : (b + 1) * LANES]
 
 
 def finish_group(where, particular, lower, upper, traces, old, first, kz_local):
@@ -384,16 +412,16 @@
     return pl.pallas_call(
         functools.partial(finish_kernel, first, kz_local, n_sub, has_old),
         out_shape=jax.ShapeDtypeStruct(total, F32),
-        grid=(waves // CHUNK,),
+        grid=(waves // CHUNK, Y_PARTS),
         in_specs=[
             scalar_spec(),
-            pl.BlockSpec((CHUNK, cheb, 2 * count), lambda i: (i, 0, 0)),
-            pl.BlockSpec((CHUNK, cheb, count), lambda i: (first + i, 0, 0)),
-            pl.BlockSpec((CHUNK, cheb, count), lambda i: (first + i, 0, 0)),
+            pl.BlockSpec((CHUNK, cheb // Y_PARTS, 2 * count), lambda i, j: (i, j, 0)),
+            pl.BlockSpec((CHUNK, cheb // Y_PARTS, count), lambda i, j: (first + i, j, 0)),
+            pl.BlockSpec((CHUNK, cheb // Y_PARTS, count), lambda i, j: (first + i, j, 0)),
         ]
-        + [pl.BlockSpec(traces[0].shape, lambda i: (0, 0, 0))] * n_sub
+        + [pl.BlockSpec(traces[0].shape, lambda i, j: (0, 0, 0))] * n_sub
         + [pl.BlockSpec(memory_space=pl.ANY)] * has_old,
-        out_specs=pl.BlockSpec((cheb, width, LANES), lambda i: (0, first + i, 0)),
+        out_specs=pl.BlockSpec((cheb // Y_PARTS, width, LANES), lambda i, j: (j, first + i, 0)),
         scratch_shapes=[
             pltpu.VMEM((n_sub, 2, 2 * waves, count), F32),
             pltpu.VMEM((n_sub + 1, 2 * waves, count), F32),
@@ -443,7 +471,7 @@
         return got, flying
 
     everything = list(range(chunks))
-    (head,) = span_part(fields, span_table, where, 0, HEAD_ROWS, [(HEAD_JOINED, everything)], 8)
+    (head,) = span_part(fields, span_table, where, 0, HEAD_ROWS, [(HEAD_JOINED, everything)], HEAD_BLOCK)
     sets = list(zip(JOINED, groups))
     bodies = span_part(fields, span_table, where, HEAD_ROWS, cheb - HEAD_ROWS, sets, BODY_BLOCK)
     head, before = (joined_exchange if HEAD_JOINED else apart_exchange)(head)
@@ -451,7 +479,7 @@
     arrived = []
     for at, value in enumerate(bodies):
         if at:
-            value, lower, upper, _ = lax.optimization_barrier((value, lower, upper, before[AFTER]))
+            value, lower, upper, _ = lax.optimization_barrier((value, lower, upper, before[:AFTER]))
         value, before = (joined_exchange if JOINED[at] else apart_exchange)(value)
         arrived.append(value)
 

time: 127 us -> 124 us (0.976)
  Pallas kernels: 64.3 us -> 57.3 us
  local copies, waits for them, and re-layouts: 3.61 us -> 5.96 us
  starting transfers between devices: 25 us -> 26.7 us
    ppermute x7, waiting for transfers between devices: 33 us -> 27.9 us  [apart_exchange(): got[step] = lax.ppermute(values[step], 'modes', pairs)]
    all_to_all x2, waiting for transfers between devices: 0.01 us -> 5.1 us  [joined_exchange(): got = lax.all_to_all(value, 'modes', 0, 0, tiled=True)]
    unnamed x24 -> x22, local copies, waits for them, and re-layouts: 2.3 us -> 5.85 us
    pallas_call x2, Pallas kernels: 29.5 us -> 26.1 us  [stream_group(): pl.pallas_call(functools.partial(stream_kernel, modes_count, parts, first...]
    ppermute x6, starting transfers between devices: 8.59 us -> 10.4 us  [chunked(): lax.ppermute(traces, 'sub', [(d, (d + shift) % n_sub) for d in range(n_su...]
    pallas_call x2, Pallas kernels: 16.5 us -> 15 us  [span_part(): pl.pallas_call(functools.partial(span_kernel, modes_count, sets, block),...]
    pallas_call x2, Pallas kernels: 13.6 us -> 12.3 us  [finish_group(): pl.pallas_call(functools.partial(finish_kernel, first, kz_local, n_sub, h...]
  transfers between devices with their start and end apart: 15 -> 15, of which waited for: 3 -> 5; matrix products, arithmetic and copies ran while one was open for 1% -> 0% of each run, Pallas kernels for 42% -> 37%
where the time goes in v1:
time: 124 us; the launch traced here: 123 us
  Pallas kernels  57.3 us (46%)
  waiting for transfers between devices  33 us (27%)
  starting transfers between devices  26.7 us (22%)
  local copies, waits for them, and re-layouts  5.96 us (5%)
    ppermute x7, waiting for transfers between devices, apart_exchange(): got[step] = lax.ppermute(values[step], 'modes', pairs)  27.9 us
    pallas_call x2, Pallas kernels, stream_group(): pl.pallas_call(functools.partial(stream_kernel, modes_count, parts, first...  26.1 us
    pallas_call x2, Pallas kernels, span_part(): pl.pallas_call(functools.partial(span_kernel, modes_count, sets, block),...  15 us
    pallas_call x2, Pallas kernels, finish_group(): pl.pallas_call(functools.partial(finish_kernel, first, kz_local, n_sub, h...  12.3 us
    ppermute x6, starting transfers between devices, chunked(): lax.ppermute(traces, 'sub', [(d, (d + shift) % n_sub) for d in range(n_su...  10.4 us
    all_to_all x2, starting transfers between devices, joined_exchange(): got = lax.all_to_all(value, 'modes', 0, 0, tiled=True)  9.65 us
    ppermute x7, starting transfers between devices, apart_exchange(): got[step] = lax.ppermute(values[step], 'modes', pairs)  6.62 us
    unnamed x22, local copies, waits for them, and re-layouts  5.85 us
  transfers between devices with their start and end apart: 15, of which 5 were waited for; matrix products, arithmetic and copies ran while one was open for 0% of the time, Pallas kernels for 37%

profile of v1, /device:TPU:0, one launch (start us, length us, event | category | flops | bytes accessed | tf_op | source)
XLA Modules:
  0.0 123.2 jit_solution(7603987850472652639)
XLA Ops:
  0.0 0.1 pad_add_fusion.where
  0.1 0.9 copy-done.3
  1.0 5.8 %span.2 = bf16[8,4,256,128]{3,2,1,0:T(8,128)(2,1)} custom-call(s32[2]{0:T(128)S(1)} %pad_add_fusion.where, bf16[2,96,128,512]{3,2,1,0:T(8,128)(2,1)} %fields.3, bf16[8,32,512]{2,1,0:T(8,128)(2,1)S(1)} %copy-done.3), custom_call_target="tpu_custom_call" | custom-call | flops 1073741824 | bytes 10485760 | tf_op jit(solution)/shard_map/span/pallas_call | solution.py:125
  6.8 5.3 %all-to-all-start = ((bf16[8,4,256,128]{3,2,1,0:T(8,128)(2,1)}), bf16[8,4,256,128]{3,2,1,0:T(8,128)(2,1)}, u32[]{:S(2)}, u32[]{:S(2)}) async-start(bf16[8,4,256,128]{3,2,1,0:T(8,128)(2,1)} %span.2), calls=%async_computation | async-start | bytes 4194304 | tf_op jit(solution)/shard_map/all_to_all | solution.py:461
  12.1 9.2 %span.3 = (bf16[2,512,128]{2,1,0:T(8,128)(2,1)S(1)}, bf16[2,512,128]{2,1,0:T(8,128)(2,1)S(1)}, bf16[2,512,128]{2,1,0:T(8,128)(2,1)S(1)}, bf16[2,512,128]{2,1,0:T...) custom-call(s32[2]{0:T(128)S(1)} %pad_add_fusion.where, ...), custom_call_target="tpu_custom_call" | custom-call | flops 2147483648 | bytes 20971520 | tf_op jit(solution)/shard_map/span/pallas_call | solution.py:125
  21.3 3.0 %collective-permute-start = (bf16[2,512,128]{2,1,0:T(8,128)(2,1)S(1)}, bf16[2,512,128]{2,1,0:T(8,128)(2,1)S(1)}, u32[]{:S(2)}, u32[]{:S(2)}) collective-permute-start(bf16[2,512,128]{2,1,0:T(8,128)(2,1)S(1)} %get-tuple-element.26), channel_id=1, source_target_pairs={{0,24},{4,28},{8,16},{12,20},{16,8},{20,12},{24,0},{28,4},{1,25},{... | collective-permute-start | bytes 786440 | tf_op jit(solution)/shard_map/ppermute | solution.py:469
  24.3 0.0 collective-permute-start.1
  24.4 1.4 %collective-permute-start.2 = (bf16[2,512,128]{2,1,0:T(8,128)(2,1)S(1)}, bf16[2,512,128]{2,1,0:T(8,128)(2,1)S(1)}, u32[]{:S(2)}, u32[]{:S(2)}) collective-permute-start(bf16[2,512,128]{2,1,0:T(8,128)(2,1)S(1)} %get-tuple-element.28), channel_id=1, source_target_pairs={{0,8},{4,12},{8,0},{12,4},{16,24},{20,28},{24,16},{28,20},{1,9},{5... | collective-permute-start | bytes 786440 | tf_op jit(solution)/shard_map/ppermute | solution.py:469
  25.7 1.5 %collective-permute-start.3 = (bf16[2,512,128]{2,1,0:T(8,128)(2,1)S(1)}, bf16[2,512,128]{2,1,0:T(8,128)(2,1)S(1)}, u32[]{:S(2)}, u32[]{:S(2)}) collective-permute-start(bf16[2,512,128]{2,1,0:T(8,128)(2,1)S(1)} %get-tuple-element.29), channel_id=1, source_target_pairs={{0,16},{4,20},{8,24},{12,28},{16,0},{20,4},{24,8},{28,12},{1,17},{... | collective-permute-start | bytes 786440 | tf_op jit(solution)/shard_map/ppermute | solution.py:469
  27.2 0.4 collective-permute-start.4
  27.6 17.4 %collective-permute-done.rest_7_ = bf16[2,512,128]{2,1,0:T(8,128)(2,1)S(1)} collective-permute-done((bf16[2,512,128]{2,1,0:T(8,128)(2,1)S(1)}, bf16[2,512,128]{2,1,0:T(8,128)(2,1)S(1)}, u32[]{:S(2)}, u32[]{:S(2)}) %collective-permute-start) | collective-permute-done | bytes 262176 | tf_op jit(solution)/shard_map/ppermute | solution.py:469
  45.0 4.0 %wall.1 = (f32[16,96,512]{2,1,0:T(8,128)S(1)}, f32[16,96,512]{2,1,0:T(8,128)}) custom-call(s32[2]{0:T(128)S(1)} %pad_add_fusion.where), custom_call_target="tpu_custom_call" | custom-call | flops 16777216 | bytes 6291456 | tf_op jit(solution)/shard_map/wall/pallas_call | solution.py:338
  49.0 1.7 %copy-done = f32[16,96,512]{2,1,0:T(8,128)} copy-done((f32[16,96,512]{2,1,0:T(8,128)}, f32[16,96,512]{2,1,0:T(8,128)S(1)}, u32[]{:S(2)}) %copy-start) | copy-done | bytes 3145752
  50.7 4.5 %collective-permute-done.2.rest_3_ = bf16[2,512,128]{2,1,0:T(8,128)(2,1)S(1)} collective-permute-done((bf16[2,512,128]{2,1,0:T(8,128)(2,1)S(1)}, bf16[2,512,128]{2,1,0:T(8,128)(2,1)S(1)}, u32[]{:S(2)}, u32[]{:S(2)}) %collective-permute-start.2) | collective-permute-done | bytes 262176 | tf_op jit(solution)/shard_map/ppermute | solution.py:469
  55.2 4.7 %collective-permute-done.4.rest_4_ = bf16[2,512,128]{2,1,0:T(8,128)(2,1)S(1)} collective-permute-done((bf16[2,512,128]{2,1,0:T(8,128)(2,1)S(1)}, bf16[2,512,128]{2,1,0:T(8,128)(2,1)S(1)}, u32[]{:S(2)}, u32[]{:S(2)}) %collective-permute-start.4) | collective-permute-done | bytes 262176 | tf_op jit(solution)/shard_map/ppermute | solution.py:469
  59.9 4.3 %all-to-all-start.1 = ((bf16[8,2,512,128]{3,2,1,0:T(8,128)(2,1)}), bf16[8,2,512,128]{3,2,1,0:T(8,128)(2,1)}, u32[]{:S(2)}, u32[]{:S(2)}) async-start(bf16[8,2,512,128]{3,2,1,0:T(8,128)(2,1)} %get-tuple-element.32), calls=%async_computation.1 | async-start | bytes 4194304 | tf_op jit(solution)/shard_map/all_to_all | solution.py:461
  64.3 0.4 collective-permute-start.9
  64.6 0.1 copy.11.lam
  64.8 1.3 %collective-permute-done.9.rest_2_ = bf16[2,512,128]{2,1,0:T(8,128)(2,1)S(1)} collective-permute-done((bf16[2,512,128]{2,1,0:T(8,128)(2,1)S(1)}, bf16[2,512,128]{2,1,0:T(8,128)(2,1)S(1)}, u32[]{:S(2)}, u32[]{:S(2)}) %collective-permute-start.9) | collective-permute-done | bytes 262176 | tf_op jit(solution)/shard_map/ppermute | solution.py:469
  66.0 0.8 copy-done.6
  66.8 13.7 %stream.3 = (f32[8,96,1024]{2,1,0:T(8,128)}, f32[2,16,512]{2,1,0:T(8,128)S(1)}) custom-call(s32[2]{0:T(128)S(1)} %pad_add_fusion.where, f32[96,128,128]{2,1,0:T(8,128)} %bitcast.22, bf16[8,128,1024]{2,1,0:T(8,128)(2,1)} %constant.17.clone.table_ref, f32[96,96]{1,0:T(8,128)S(1)} %bitcast.16, f32[96,96]{1,0:T(8,128)S(1)} %bitcast.18, f32[8,96]{1,0:T(8,128)S(1)} %pad.4.e_ref, ...), custom_call_target="tpu_custom_call" | custom-call | flops 6442450944 | bytes 4194304 | tf_op jit(solution)/shard_map/stream/pallas_call | solution.py:295
  80.6 0.0 copy-start.2
  80.6 4.2 %collective-permute-start.12 = (f32[2,16,512]{2,1,0:T(8,128)S(1)}, f32[2,16,512]{2,1,0:T(8,128)S(1)}, u32[]{:S(2)}, u32[]{:S(2)}) collective-permute-start(f32[2,16,512]{2,1,0:T(8,128)S(1)} %get-tuple-element.40.rest_0_), channel_id=1, source_target_pairs={{0,3},{1,0},{2,1},{3,2},{4,7},{5,4},{6,5},{7,6},{8,11},{9,8},{10,9... | collective-permute-start | bytes 196616 | tf_op jit(solution)/shard_map/ppermute | solution.py:493
  84.8 1.0 collective-permute-start.10
  85.8 5.1 %all-to-all-done.1.rest_1_ = bf16[8,2,512,128]{3,2,1,0:T(8,128)(2,1)} async-done(((bf16[8,2,512,128]{3,2,1,0:T(8,128)(2,1)}), bf16[8,2,512,128]{3,2,1,0:T(8,128)(2,1)}, u32[]{:S(2)}, u32[]{:S(2)}) %all-to-all-start.1) | async-done | bytes 2097184 | tf_op jit(solution)/shard_map/all_to_all | solution.py:461
  90.9 0.8 copy-done.7
  91.7 1.6 %copy-done.8 = bf16[8,128,1024]{2,1,0:T(8,128)(2,1)S(1)} copy-done((bf16[8,128,1024]{2,1,0:T(8,128)(2,1)S(1)}, bf16[8,128,1024]{2,1,0:T(8,128)(2,1)}, u32[]{:S(2)}) %copy-start.8) | copy-done | bytes 2097176
  93.3 12.3 %stream.2 = (f32[8,96,1024]{2,1,0:T(8,128)}, f32[2,16,512]{2,1,0:T(8,128)S(1)}) custom-call(s32[2]{0:T(128)S(1)} %pad_add_fusion.where, f32[96,128,128]{2,1,0:T(8,128)} %bitcast.23, bf16[8,128,1024]{2,1,0:T(8,128)(2,1)S(1)} %copy-done.8, f32[96,96]{1,0:T(8,128)S(1)} %bitcast.17, f32[96,96]{1,0:T(8,128)S(1)} %bitcast.19, f32[8,96]{1,0:T(8,128)S(1)} %pad.4.e_ref, ...), custom_call_target="tpu_custom_call" | custom-call | flops 6442450944 | bytes 4194304 | tf_op jit(solution)/shard_map/stream/pallas_call | solution.py:295
  105.6 4.2 %collective-permute-start.8 = (f32[2,16,512]{2,1,0:T(8,128)S(1)}, f32[2,16,512]{2,1,0:T(8,128)S(1)}, u32[]{:S(2)}, u32[]{:S(2)}) collective-permute-start(f32[2,16,512]{2,1,0:T(8,128)S(1)} %get-tuple-element.36.rest_0_), channel_id=1, source_target_pairs={{0,3},{1,0},{2,1},{3,2},{4,7},{5,4},{6,5},{7,6},{8,11},{9,8},{10,9... | collective-permute-start | bytes 196616 | tf_op jit(solution)/shard_map/ppermute | solution.py:493
  109.8 1.0 collective-permute-start.6
  110.9 6.2 %finish.2.rest_4_ = f32[96,128,128]{2,1,0:T(8,128)} custom-call(s32[2]{0:T(128)S(1)} %pad_add_fusion.where, f32[8,96,1024]{2,1,0:T(8,128)S(1)} %copy-done.2, f32[16,96,512]{2,1,0:T(8,128)} %copy-done, f32[16,96,512]{2,1,0:T(8,128)} %get-tuple-element.35.upper, f32[2,16,512]{2,1,0:T(8,128)S(1)} %get-tuple-element.40.rest_0_, ...), custom_call_target="tpu_custom_call" | custom-call | flops 4194304 | bytes 4194304 | tf_op jit(solution)/shard_map/finish/pallas_call | solution.py:412
  117.1 6.1 %finish.3 = f32[96,128,128]{2,1,0:T(8,128)} custom-call(s32[2]{0:T(128)S(1)} %pad_add_fusion.where, f32[8,96,1024]{2,1,0:T(8,128)S(1)} %copy-done.1, f32[16,96,512]{2,1,0:T(8,128)} %copy-done, f32[16,96,512]{2,1,0:T(8,128)} %get-tuple-element.35.upper, f32[2,16,512]{2,1,0:T(8,128)S(1)} %get-tuple-element.36.rest_0_, ...), custom_call_target="tpu_custom_call", output_to_operand_aliasing={{}: (8, {})} | custom-call | flops 4194304 | bytes 4194304 | tf_op jit(solution)/shard_map/finish/pallas_call | solution.py:412
  (30 shorter events, 0.1 us)
Async XLA Ops:
  0.1 0.9 copy-start.3
  6.8 5.3 %copy-start.4 = (bf16[8,32,512]{2,1,0:T(8,128)(2,1)S(1)}, bf16[8,32,512]{2,1,0:T(8,128)(2,1)}, u32[]{:S(2)}) copy-start(bf16[8,32,512]{2,1,0:T(8,128)(2,1)} %constant.16.clone.table) | copy-start | bytes 786436
  6.8 53.1 %all-to-all-start = ((bf16[8,4,256,128]{3,2,1,0:T(8,128)(2,1)}), bf16[8,4,256,128]{3,2,1,0:T(8,128)(2,1)}, u32[]{:S(2)}, u32[]{:S(2)}) async-start(bf16[8,4,256,128]{3,2,1,0:T(8,128)(2,1)} %span.2), calls=%async_computation | async-start | bytes 4194304 | tf_op jit(solution)/shard_map/all_to_all | solution.py:461
  21.3 23.7 %collective-permute-start = (bf16[2,512,128]{2,1,0:T(8,128)(2,1)S(1)}, bf16[2,512,128]{2,1,0:T(8,128)(2,1)S(1)}, u32[]{:S(2)}, u32[]{:S(2)}) collective-permute-start(bf16[2,512,128]{2,1,0:T(8,128)(2,1)S(1)} %get-tuple-element.26), channel_id=1, source_target_pairs={{0,24},{4,28},{8,16},{12,20},{16,8},{20,12},{24,0},{28,4},{1,25},{... | collective-permute-start | bytes 786440 | tf_op jit(solution)/shard_map/ppermute | solution.py:469
  24.3 26.3 %collective-permute-start.1 = (bf16[2,512,128]{2,1,0:T(8,128)(2,1)S(1)}, bf16[2,512,128]{2,1,0:T(8,128)(2,1)S(1)}, u32[]{:S(2)}, u32[]{:S(2)}) collective-permute-start(bf16[2,512,128]{2,1,0:T(8,128)(2,1)S(1)} %get-tuple-element.27), channel_id=1, source_target_pairs={{0,28},{4,24},{8,20},{12,16},{16,12},{20,8},{24,4},{28,0},{1,29},{... | collective-permute-start | bytes 786440 | tf_op jit(solution)/shard_map/ppermute | solution.py:469
  24.4 30.9 %collective-permute-start.2 = (bf16[2,512,128]{2,1,0:T(8,128)(2,1)S(1)}, bf16[2,512,128]{2,1,0:T(8,128)(2,1)S(1)}, u32[]{:S(2)}, u32[]{:S(2)}) collective-permute-start(bf16[2,512,128]{2,1,0:T(8,128)(2,1)S(1)} %get-tuple-element.28), channel_id=1, source_target_pairs={{0,8},{4,12},{8,0},{12,4},{16,24},{20,28},{24,16},{28,20},{1,9},{5... | collective-permute-start | bytes 786440 | tf_op jit(solution)/shard_map/ppermute | solution.py:469
  25.7 29.5 %collective-permute-start.3 = (bf16[2,512,128]{2,1,0:T(8,128)(2,1)S(1)}, bf16[2,512,128]{2,1,0:T(8,128)(2,1)S(1)}, u32[]{:S(2)}, u32[]{:S(2)}) collective-permute-start(bf16[2,512,128]{2,1,0:T(8,128)(2,1)S(1)} %get-tuple-element.29), channel_id=1, source_target_pairs={{0,16},{4,20},{8,24},{12,28},{16,0},{20,4},{24,8},{28,12},{1,17},{... | collective-permute-start | bytes 786440 | tf_op jit(solution)/shard_map/ppermute | solution.py:469
  27.2 32.7 %collective-permute-start.4 = (bf16[2,512,128]{2,1,0:T(8,128)(2,1)S(1)}, bf16[2,512,128]{2,1,0:T(8,128)(2,1)S(1)}, u32[]{:S(2)}, u32[]{:S(2)}) collective-permute-start(bf16[2,512,128]{2,1,0:T(8,128)(2,1)S(1)} %get-tuple-element.30), channel_id=1, source_target_pairs={{0,12},{4,8},{8,4},{12,0},{16,28},{20,24},{24,20},{28,16},{1,13},{... | collective-permute-start | bytes 786440 | tf_op jit(solution)/shard_map/ppermute | solution.py:469
  45.0 19.6 %copy-start.10 = (f32[96]{0:T(128)S(1)}, f32[96]{0:T(128)}, u32[]{:S(2)}) copy-start(f32[96]{0:T(128)} %param.12) | copy-start | bytes 1156
  45.0 19.8 %copy-start.9 = (f32[1,2,96]{2,1,0:T(2,128)S(1)}, f32[1,2,96]{2,1,0:T(2,128)}, u32[]{:S(2)}) copy-start(f32[1,2,96]{2,1,0:T(2,128)} %param.13) | copy-start | bytes 2308
  45.0 21.0 %copy-start.5 = (f32[1,96,96]{2,1,0:T(8,128)S(1)}, f32[1,96,96]{2,1,0:T(8,128)}, u32[]{:S(2)}) copy-start(f32[1,96,96]{2,1,0:T(8,128)} %param.11) | copy-start | bytes 110596
  45.0 14.9 %collective-permute-start.5 = (bf16[2,512,128]{2,1,0:T(8,128)(2,1)S(1)}, bf16[2,512,128]{2,1,0:T(8,128)(2,1)S(1)}, u32[]{:S(2)}, u32[]{:S(2)}) collective-permute-start(bf16[2,512,128]{2,1,0:T(8,128)(2,1)S(1)} %get-tuple-element.31), channel_id=1, source_target_pairs={{0,20},{4,16},{8,28},{12,24},{16,4},{20,0},{24,12},{28,8},{1,21},{... | collective-permute-start | bytes 786440 | tf_op jit(solution)/shard_map/ppermute | solution.py:469
  49.0 1.7 %copy-start = (f32[16,96,512]{2,1,0:T(8,128)}, f32[16,96,512]{2,1,0:T(8,128)S(1)}, u32[]{:S(2)}) copy-start(f32[16,96,512]{2,1,0:T(8,128)S(1)} %get-tuple-element.34.lower) | copy-start | bytes 9437188
  59.9 31.0 %all-to-all-start.1 = ((bf16[8,2,512,128]{3,2,1,0:T(8,128)(2,1)}), bf16[8,2,512,128]{3,2,1,0:T(8,128)(2,1)}, u32[]{:S(2)}, u32[]{:S(2)}) async-start(bf16[8,2,512,128]{3,2,1,0:T(8,128)(2,1)} %get-tuple-element.32), calls=%async_computation.1 | async-start | bytes 4194304 | tf_op jit(solution)/shard_map/all_to_all | solution.py:461
  64.3 1.8 %collective-permute-start.9 = (bf16[2,512,128]{2,1,0:T(8,128)(2,1)S(1)}, bf16[2,512,128]{2,1,0:T(8,128)(2,1)S(1)}, u32[]{:S(2)}, u32[]{:S(2)}) collective-permute-start(bf16[2,512,128]{2,1,0:T(8,128)(2,1)S(1)} %get-tuple-element.38), channel_id=1, source_target_pairs={{0,4},{4,0},{8,12},{12,8},{16,20},{20,16},{24,28},{28,24},{1,5},{5... | collective-permute-start | bytes 786440 | tf_op jit(solution)/shard_map/ppermute | solution.py:469
  66.0 0.8 copy-start.6
  80.6 30.3 %copy-start.2 = (f32[8,96,1024]{2,1,0:T(8,128)S(1)}, f32[8,96,1024]{2,1,0:T(8,128)}, u32[]{:S(2)}) copy-start(f32[8,96,1024]{2,1,0:T(8,128)} %get-tuple-element.39.particular) | copy-start | bytes 9437188
  80.6 29.2 %collective-permute-start.12 = (f32[2,16,512]{2,1,0:T(8,128)S(1)}, f32[2,16,512]{2,1,0:T(8,128)S(1)}, u32[]{:S(2)}, u32[]{:S(2)}) collective-permute-start(f32[2,16,512]{2,1,0:T(8,128)S(1)} %get-tuple-element.40.rest_0_), channel_id=1, source_target_pairs={{0,3},{1,0},{2,1},{3,2},{4,7},{5,4},{6,5},{7,6},{8,11},{9,8},{10,9... | collective-permute-start | bytes 196616 | tf_op jit(solution)/shard_map/ppermute | solution.py:493
  84.8 26.1 %collective-permute-start.11 = (f32[2,16,512]{2,1,0:T(8,128)S(1)}, f32[2,16,512]{2,1,0:T(8,128)S(1)}, u32[]{:S(2)}, u32[]{:S(2)}) collective-permute-start(f32[2,16,512]{2,1,0:T(8,128)S(1)} %get-tuple-element.40.rest_0_), channel_id=1, source_target_pairs={{0,2},{1,3},{2,0},{3,1},{4,6},{5,7},{6,4},{7,5},{8,10},{9,11},{10,... | collective-permute-start | bytes 196616 | tf_op jit(solution)/shard_map/ppermute | solution.py:493
  84.8 26.1 %collective-permute-start.10 = (f32[2,16,512]{2,1,0:T(8,128)S(1)}, f32[2,16,512]{2,1,0:T(8,128)S(1)}, u32[]{:S(2)}, u32[]{:S(2)}) collective-permute-start(f32[2,16,512]{2,1,0:T(8,128)S(1)} %get-tuple-element.40.rest_0_), channel_id=1, source_target_pairs={{0,1},{1,2},{2,3},{3,0},{4,5},{5,6},{6,7},{7,4},{8,9},{9,10},{10,1... | collective-permute-start | bytes 196616 | tf_op jit(solution)/shard_map/ppermute | solution.py:493
  90.9 0.8 copy-start.7
  91.7 1.6 %copy-start.8 = (bf16[8,128,1024]{2,1,0:T(8,128)(2,1)S(1)}, bf16[8,128,1024]{2,1,0:T(8,128)(2,1)}, u32[]{:S(2)}) copy-start(bf16[8,128,1024]{2,1,0:T(8,128)(2,1)} %constant.17.clone.table_ref) | copy-start | bytes 6291460
  105.6 11.4 %collective-permute-start.8 = (f32[2,16,512]{2,1,0:T(8,128)S(1)}, f32[2,16,512]{2,1,0:T(8,128)S(1)}, u32[]{:S(2)}, u32[]{:S(2)}) collective-permute-start(f32[2,16,512]{2,1,0:T(8,128)S(1)} %get-tuple-element.36.rest_0_), channel_id=1, source_target_pairs={{0,3},{1,0},{2,1},{3,2},{4,7},{5,4},{6,5},{7,6},{8,11},{9,8},{10,9... | collective-permute-start | bytes 196616 | tf_op jit(solution)/shard_map/ppermute | solution.py:493
  109.8 7.2 %collective-permute-start.7 = (f32[2,16,512]{2,1,0:T(8,128)S(1)}, f32[2,16,512]{2,1,0:T(8,128)S(1)}, u32[]{:S(2)}, u32[]{:S(2)}) collective-permute-start(f32[2,16,512]{2,1,0:T(8,128)S(1)} %get-tuple-element.36.rest_0_), channel_id=1, source_target_pairs={{0,2},{1,3},{2,0},{3,1},{4,6},{5,7},{6,4},{7,5},{8,10},{9,11},{10,... | collective-permute-start | bytes 196616 | tf_op jit(solution)/shard_map/ppermute | solution.py:493
  109.8 7.2 %collective-permute-start.6 = (f32[2,16,512]{2,1,0:T(8,128)S(1)}, f32[2,16,512]{2,1,0:T(8,128)S(1)}, u32[]{:S(2)}, u32[]{:S(2)}) collective-permute-start(f32[2,16,512]{2,1,0:T(8,128)S(1)} %get-tuple-element.36.rest_0_), channel_id=1, source_target_pairs={{0,1},{1,2},{2,3},{3,0},{4,5},{5,6},{6,7},{7,4},{8,9},{9,10},{10,1... | collective-permute-start | bytes 196616 | tf_op jit(solution)/shard_map/ppermute | solution.py:493
  110.9 6.2 %copy-start.1 = (f32[8,96,1024]{2,1,0:T(8,128)S(1)}, f32[8,96,1024]{2,1,0:T(8,128)}, u32[]{:S(2)}) copy-start(f32[8,96,1024]{2,1,0:T(8,128)} %get-tuple-element.33.particular) | copy-start | bytes 9437188

commit v2 on v1

--- a/solution.py
+++ b/solution.py
@@ -215,12 +215,13 @@
     extended = cheb + end_map.shape[0]
 
     for place in range(size):
-        for copy in copies(place):
-            copy.wait()
         if place == 0:
             table_copy.wait()
+        landing = copies(place)
         row = 0
-        for arrays, _, rows in parts:
+        for part, (arrays, _, rows) in enumerate(parts):
+            for copy in landing[part * modes_count : (part + 1) * modes_count]:
+                copy.wait()
             origin = [d if arrays == 1 else me ^ d for d in range(modes_count)]
             base = row
 
@@ -341,7 +342,7 @@
         grid=(kz_local // CHUNK,),
         in_specs=[scalar_spec()],
         out_specs=[pl.BlockSpec((CHUNK, cheb, count), lambda i: (i, 0, 0))] * 2,
-        compiler_params=params(),
+        compiler_params=params(58 * 1024 * 1024),
         cost_estimate=pl.CostEstimate(flops=1 << 24, bytes_accessed=6 << 20, transcendentals=2 << 20),
         name="wall",
     )(where)

time: 124 us -> 123 us (level)
  local copies, waits for them, and re-layouts: 5.96 us -> 4.28 us
    unnamed x22 -> x24, local copies, waits for them, and re-layouts: 5.85 us -> 4.17 us
where the time goes in v2:
time: 123 us
  Pallas kernels  57.9 us (47%)
  waiting for transfers between devices  33.7 us (27%)
  starting transfers between devices  26.7 us (22%)
  local copies, waits for them, and re-layouts  4.28 us (3%)
    ppermute x7, waiting for transfers between devices, apart_exchange(): got[step] = lax.ppermute(values[step], 'modes', pairs)  28.6 us
    pallas_call x2, Pallas kernels, stream_group(): pl.pallas_call(functools.partial(stream_kernel, modes_count, parts, first...  25.7 us
    pallas_call x2, Pallas kernels, span_part(): pl.pallas_call(functools.partial(span_kernel, modes_count, sets, block),...  15 us
    pallas_call x2, Pallas kernels, finish_group(): pl.pallas_call(functools.partial(finish_kernel, first, kz_local, n_sub, h...  12.3 us
    ppermute x6, starting transfers between devices, chunked(): lax.ppermute(traces, 'sub', [(d, (d + shift) % n_sub) for d in range(n_su...  10.4 us
    all_to_all x2, starting transfers between devices, joined_exchange(): got = lax.all_to_all(value, 'modes', 0, 0, tiled=True)  9.65 us
    ppermute x7, starting transfers between devices, apart_exchange(): got[step] = lax.ppermute(values[step], 'modes', pairs)  6.67 us
    all_to_all x2, waiting for transfers between devices, joined_exchange(): got = lax.all_to_all(value, 'modes', 0, 0, tiled=True)  5.1 us
  transfers between devices with their start and end apart: 15, of which 5 were waited for; matrix products, arithmetic and copies ran while one was open for 0% of the time, Pallas kernels for 37%

profile of v2, /device:TPU:0, one launch (start us, length us, event | category | flops | bytes accessed | tf_op | source)
XLA Modules:
  0.0 122.8 jit_solution(6720054752004869992)
XLA Ops:
  0.0 0.1 pad_add_fusion.where
  0.1 0.9 copy-done.2
  1.0 5.8 %span.2 = bf16[8,4,256,128]{3,2,1,0:T(8,128)(2,1)} custom-call(s32[2]{0:T(128)S(1)} %pad_add_fusion.where, bf16[2,96,128,512]{3,2,1,0:T(8,128)(2,1)} %fields.3, bf16[8,32,512]{2,1,0:T(8,128)(2,1)S(1)} %copy-done.2), custom_call_target="tpu_custom_call" | custom-call | flops 1073741824 | bytes 10485760 | tf_op jit(solution)/shard_map/span/pallas_call | solution.py:125
  6.8 5.3 %all-to-all-start = ((bf16[8,4,256,128]{3,2,1,0:T(8,128)(2,1)}), bf16[8,4,256,128]{3,2,1,0:T(8,128)(2,1)}, u32[]{:S(2)}, u32[]{:S(2)}) async-start(bf16[8,4,256,128]{3,2,1,0:T(8,128)(2,1)} %span.2), calls=%async_computation | async-start | bytes 4194304 | tf_op jit(solution)/shard_map/all_to_all | solution.py:462
  12.1 9.2 %span.3 = (bf16[2,512,128]{2,1,0:T(8,128)(2,1)S(1)}, bf16[2,512,128]{2,1,0:T(8,128)(2,1)S(1)}, bf16[2,512,128]{2,1,0:T(8,128)(2,1)S(1)}, bf16[2,512,128]{2,1,0:T...) custom-call(s32[2]{0:T(128)S(1)} %pad_add_fusion.where, ...), custom_call_target="tpu_custom_call" | custom-call | flops 2147483648 | bytes 20971520 | tf_op jit(solution)/shard_map/span/pallas_call | solution.py:125
  21.4 3.0 %collective-permute-start = (bf16[2,512,128]{2,1,0:T(8,128)(2,1)S(1)}, bf16[2,512,128]{2,1,0:T(8,128)(2,1)S(1)}, u32[]{:S(2)}, u32[]{:S(2)}) collective-permute-start(bf16[2,512,128]{2,1,0:T(8,128)(2,1)S(1)} %get-tuple-element.26), channel_id=1, source_target_pairs={{0,24},{4,28},{8,16},{12,20},{16,8},{20,12},{24,0},{28,4},{1,25},{... | collective-permute-start | bytes 786440 | tf_op jit(solution)/shard_map/ppermute | solution.py:470
  24.4 0.0 collective-permute-start.1
  24.4 1.4 %collective-permute-start.2 = (bf16[2,512,128]{2,1,0:T(8,128)(2,1)S(1)}, bf16[2,512,128]{2,1,0:T(8,128)(2,1)S(1)}, u32[]{:S(2)}, u32[]{:S(2)}) collective-permute-start(bf16[2,512,128]{2,1,0:T(8,128)(2,1)S(1)} %get-tuple-element.28), channel_id=1, source_target_pairs={{0,8},{4,12},{8,0},{12,4},{16,24},{20,28},{24,16},{28,20},{1,9},{5... | collective-permute-start | bytes 786440 | tf_op jit(solution)/shard_map/ppermute | solution.py:470
  25.8 1.5 %collective-permute-start.3 = (bf16[2,512,128]{2,1,0:T(8,128)(2,1)S(1)}, bf16[2,512,128]{2,1,0:T(8,128)(2,1)S(1)}, u32[]{:S(2)}, u32[]{:S(2)}) collective-permute-start(bf16[2,512,128]{2,1,0:T(8,128)(2,1)S(1)} %get-tuple-element.29), channel_id=1, source_target_pairs={{0,16},{4,20},{8,24},{12,28},{16,0},{20,4},{24,8},{28,12},{1,17},{... | collective-permute-start | bytes 786440 | tf_op jit(solution)/shard_map/ppermute | solution.py:470
  27.3 0.4 collective-permute-start.4
  27.6 17.4 %collective-permute-done.rest_7_ = bf16[2,512,128]{2,1,0:T(8,128)(2,1)S(1)} collective-permute-done((bf16[2,512,128]{2,1,0:T(8,128)(2,1)S(1)}, bf16[2,512,128]{2,1,0:T(8,128)(2,1)S(1)}, u32[]{:S(2)}, u32[]{:S(2)}) %collective-permute-start) | collective-permute-done | bytes 262176 | tf_op jit(solution)/shard_map/ppermute | solution.py:470
  45.0 0.1 collective-permute-start.5
  45.1 4.9 %wall.1 = (f32[16,96,512]{2,1,0:T(8,128)}, f32[16,96,512]{2,1,0:T(8,128)}) custom-call(s32[2]{0:T(128)} %copy-done.4), custom_call_target="tpu_custom_call" | custom-call | flops 16777216 | bytes 6291456 | tf_op jit(solution)/shard_map/wall/pallas_call | solution.py:339
  50.0 5.3 %collective-permute-done.2.rest_3_ = bf16[2,512,128]{2,1,0:T(8,128)(2,1)S(1)} collective-permute-done((bf16[2,512,128]{2,1,0:T(8,128)(2,1)S(1)}, bf16[2,512,128]{2,1,0:T(8,128)(2,1)S(1)}, u32[]{:S(2)}, u32[]{:S(2)}) %collective-permute-start.2) | collective-permute-done | bytes 262176 | tf_op jit(solution)/shard_map/ppermute | solution.py:470
  55.2 4.6 %collective-permute-done.4.rest_4_ = bf16[2,512,128]{2,1,0:T(8,128)(2,1)S(1)} collective-permute-done((bf16[2,512,128]{2,1,0:T(8,128)(2,1)S(1)}, bf16[2,512,128]{2,1,0:T(8,128)(2,1)S(1)}, u32[]{:S(2)}, u32[]{:S(2)}) %collective-permute-start.4) | collective-permute-done | bytes 262176 | tf_op jit(solution)/shard_map/ppermute | solution.py:470
  59.9 4.3 %all-to-all-start.1 = ((bf16[8,2,512,128]{3,2,1,0:T(8,128)(2,1)}), bf16[8,2,512,128]{3,2,1,0:T(8,128)(2,1)}, u32[]{:S(2)}, u32[]{:S(2)}) async-start(bf16[8,2,512,128]{3,2,1,0:T(8,128)(2,1)} %get-tuple-element.32), calls=%async_computation.1 | async-start | bytes 4194304 | tf_op jit(solution)/shard_map/all_to_all | solution.py:462
  64.3 0.4 collective-permute-start.9
  64.6 0.1 copy.11.lam
  64.8 1.3 %collective-permute-done.9.rest_2_ = bf16[2,512,128]{2,1,0:T(8,128)(2,1)S(1)} collective-permute-done((bf16[2,512,128]{2,1,0:T(8,128)(2,1)S(1)}, bf16[2,512,128]{2,1,0:T(8,128)(2,1)S(1)}, u32[]{:S(2)}, u32[]{:S(2)}) %collective-permute-start.9) | collective-permute-done | bytes 262176 | tf_op jit(solution)/shard_map/ppermute | solution.py:470
  66.0 0.8 copy-done.7
  66.8 13.8 %stream.3 = (f32[8,96,1024]{2,1,0:T(8,128)}, f32[2,16,512]{2,1,0:T(8,128)S(1)}) custom-call(s32[2]{0:T(128)S(1)} %copy-done.5, f32[96,128,128]{2,1,0:T(8,128)} %bitcast.22, bf16[8,128,1024]{2,1,0:T(8,128)(2,1)} %constant.17.clone.table_ref, f32[96,96]{1,0:T(8,128)S(1)} %bitcast.16, f32[96,96]{1,0:T(8,128)S(1)} %bitcast.18, f32[8,96]{1,0:T(8,128)S(1)} %pad.4.e_ref, ...), custom_call_target="tpu_custom_call" | custom-call | flops 6442450944 | bytes 4194304 | tf_op jit(solution)/shard_map/stream/pallas_call | solution.py:296
  80.6 0.0 copy-start.1
  80.6 4.2 %collective-permute-start.12 = (f32[2,16,512]{2,1,0:T(8,128)S(1)}, f32[2,16,512]{2,1,0:T(8,128)S(1)}, u32[]{:S(2)}, u32[]{:S(2)}) collective-permute-start(f32[2,16,512]{2,1,0:T(8,128)S(1)} %get-tuple-element.40.rest_0_), channel_id=1, source_target_pairs={{0,3},{1,0},{2,1},{3,2},{4,7},{5,4},{6,5},{7,6},{8,11},{9,8},{10,9... | collective-permute-start | bytes 196616 | tf_op jit(solution)/shard_map/ppermute | solution.py:494
  84.8 1.0 collective-permute-start.10
  85.8 5.1 %all-to-all-done.1.rest_1_ = bf16[8,2,512,128]{3,2,1,0:T(8,128)(2,1)} async-done(((bf16[8,2,512,128]{3,2,1,0:T(8,128)(2,1)}), bf16[8,2,512,128]{3,2,1,0:T(8,128)(2,1)}, u32[]{:S(2)}, u32[]{:S(2)}) %all-to-all-start.1) | async-done | bytes 2097184 | tf_op jit(solution)/shard_map/all_to_all | solution.py:462
  90.9 0.8 copy-done.8
  91.7 1.6 %copy-done.9 = bf16[8,128,1024]{2,1,0:T(8,128)(2,1)S(1)} copy-done((bf16[8,128,1024]{2,1,0:T(8,128)(2,1)S(1)}, bf16[8,128,1024]{2,1,0:T(8,128)(2,1)}, u32[]{:S(2)}) %copy-start.9) | copy-done | bytes 2097176
  93.3 12.0 %stream.2 = (f32[8,96,1024]{2,1,0:T(8,128)}, f32[2,16,512]{2,1,0:T(8,128)S(1)}) custom-call(s32[2]{0:T(128)S(1)} %copy-done.5, f32[96,128,128]{2,1,0:T(8,128)} %bitcast.23, bf16[8,128,1024]{2,1,0:T(8,128)(2,1)S(1)} %copy-done.9, f32[96,96]{1,0:T(8,128)S(1)} %bitcast.17, f32[96,96]{1,0:T(8,128)S(1)} %bitcast.19, f32[8,96]{1,0:T(8,128)S(1)} %pad.4.e_ref, ...), custom_call_target="tpu_custom_call" | custom-call | flops 6442450944 | bytes 4194304 | tf_op jit(solution)/shard_map/stream/pallas_call | solution.py:296
  105.3 4.2 %collective-permute-start.8 = (f32[2,16,512]{2,1,0:T(8,128)S(1)}, f32[2,16,512]{2,1,0:T(8,128)S(1)}, u32[]{:S(2)}, u32[]{:S(2)}) collective-permute-start(f32[2,16,512]{2,1,0:T(8,128)S(1)} %get-tuple-element.36.rest_0_), channel_id=1, source_target_pairs={{0,3},{1,0},{2,1},{3,2},{4,7},{5,4},{6,5},{7,6},{8,11},{9,8},{10,9... | collective-permute-start | bytes 196616 | tf_op jit(solution)/shard_map/ppermute | solution.py:494
  109.5 1.0 collective-permute-start.6
  110.5 6.2 %finish.2.rest_4_ = f32[96,128,128]{2,1,0:T(8,128)} custom-call(s32[2]{0:T(128)S(1)} %copy-done.5, f32[8,96,1024]{2,1,0:T(8,128)S(1)} %copy-done.1, f32[16,96,512]{2,1,0:T(8,128)} %get-tuple-element.34.lower, f32[16,96,512]{2,1,0:T(8,128)} %get-tuple-element.35.upper, f32[2,16,512]{2,1,0:T(8,128)S(1)} %get-tuple-element.40.rest_0_, ...), custom_call_target="tpu_custom_call" | custom-call | flops 4194304 | bytes 4194304 | tf_op jit(solution)/shard_map/finish/pallas_call | solution.py:413
  116.7 6.1 %finish.3 = f32[96,128,128]{2,1,0:T(8,128)} custom-call(s32[2]{0:T(128)S(1)} %copy-done.5, f32[8,96,1024]{2,1,0:T(8,128)S(1)} %copy-done, f32[16,96,512]{2,1,0:T(8,128)} %get-tuple-element.34.lower, f32[16,96,512]{2,1,0:T(8,128)} %get-tuple-element.35.upper, f32[2,16,512]{2,1,0:T(8,128)S(1)} %get-tuple-element.36.rest_0_, ...), custom_call_target="tpu_custom_call", output_to_operand_aliasing={{}: (8, {})} | custom-call | flops 4194304 | bytes 4194304 | tf_op jit(solution)/shard_map/finish/pallas_call | solution.py:413
  (32 shorter events, 0.1 us)
Async XLA Ops:
  0.1 0.9 copy-start.2
  1.0 11.1 %copy-start.4 = (s32[2]{0:T(128)}, s32[2]{0:T(128)S(1)}, u32[]{:S(2)}) copy-start(s32[2]{0:T(128)S(1)} %pad_add_fusion.where) | copy-start | bytes 28
  6.8 5.3 %copy-start.3 = (bf16[8,32,512]{2,1,0:T(8,128)(2,1)S(1)}, bf16[8,32,512]{2,1,0:T(8,128)(2,1)}, u32[]{:S(2)}) copy-start(bf16[8,32,512]{2,1,0:T(8,128)(2,1)} %constant.16.clone.table) | copy-start | bytes 786436
  6.8 53.1 %all-to-all-start = ((bf16[8,4,256,128]{3,2,1,0:T(8,128)(2,1)}), bf16[8,4,256,128]{3,2,1,0:T(8,128)(2,1)}, u32[]{:S(2)}, u32[]{:S(2)}) async-start(bf16[8,4,256,128]{3,2,1,0:T(8,128)(2,1)} %span.2), calls=%async_computation | async-start | bytes 4194304 | tf_op jit(solution)/shard_map/all_to_all | solution.py:462
  21.4 23.6 %collective-permute-start = (bf16[2,512,128]{2,1,0:T(8,128)(2,1)S(1)}, bf16[2,512,128]{2,1,0:T(8,128)(2,1)S(1)}, u32[]{:S(2)}, u32[]{:S(2)}) collective-permute-start(bf16[2,512,128]{2,1,0:T(8,128)(2,1)S(1)} %get-tuple-element.26), channel_id=1, source_target_pairs={{0,24},{4,28},{8,16},{12,20},{16,8},{20,12},{24,0},{28,4},{1,25},{... | collective-permute-start | bytes 786440 | tf_op jit(solution)/shard_map/ppermute | solution.py:470
  24.4 25.5 %collective-permute-start.1 = (bf16[2,512,128]{2,1,0:T(8,128)(2,1)S(1)}, bf16[2,512,128]{2,1,0:T(8,128)(2,1)S(1)}, u32[]{:S(2)}, u32[]{:S(2)}) collective-permute-start(bf16[2,512,128]{2,1,0:T(8,128)(2,1)S(1)} %get-tuple-element.27), channel_id=1, source_target_pairs={{0,28},{4,24},{8,20},{12,16},{16,12},{20,8},{24,4},{28,0},{1,29},{... | collective-permute-start | bytes 786440 | tf_op jit(solution)/shard_map/ppermute | solution.py:470
  24.4 30.8 %collective-permute-start.2 = (bf16[2,512,128]{2,1,0:T(8,128)(2,1)S(1)}, bf16[2,512,128]{2,1,0:T(8,128)(2,1)S(1)}, u32[]{:S(2)}, u32[]{:S(2)}) collective-permute-start(bf16[2,512,128]{2,1,0:T(8,128)(2,1)S(1)} %get-tuple-element.28), channel_id=1, source_target_pairs={{0,8},{4,12},{8,0},{12,4},{16,24},{20,28},{24,16},{28,20},{1,9},{5... | collective-permute-start | bytes 786440 | tf_op jit(solution)/shard_map/ppermute | solution.py:470
  25.8 29.5 %collective-permute-start.3 = (bf16[2,512,128]{2,1,0:T(8,128)(2,1)S(1)}, bf16[2,512,128]{2,1,0:T(8,128)(2,1)S(1)}, u32[]{:S(2)}, u32[]{:S(2)}) collective-permute-start(bf16[2,512,128]{2,1,0:T(8,128)(2,1)S(1)} %get-tuple-element.29), channel_id=1, source_target_pairs={{0,16},{4,20},{8,24},{12,28},{16,0},{20,4},{24,8},{28,12},{1,17},{... | collective-permute-start | bytes 786440 | tf_op jit(solution)/shard_map/ppermute | solution.py:470
  27.3 32.6 %collective-permute-start.4 = (bf16[2,512,128]{2,1,0:T(8,128)(2,1)S(1)}, bf16[2,512,128]{2,1,0:T(8,128)(2,1)S(1)}, u32[]{:S(2)}, u32[]{:S(2)}) collective-permute-start(bf16[2,512,128]{2,1,0:T(8,128)(2,1)S(1)} %get-tuple-element.30), channel_id=1, source_target_pairs={{0,12},{4,8},{8,4},{12,0},{16,28},{20,24},{24,20},{28,16},{1,13},{... | collective-permute-start | bytes 786440 | tf_op jit(solution)/shard_map/ppermute | solution.py:470
  45.0 19.6 %copy-start.11 = (f32[96]{0:T(128)S(1)}, f32[96]{0:T(128)}, u32[]{:S(2)}) copy-start(f32[96]{0:T(128)} %param.12) | copy-start | bytes 1156
  45.0 19.7 %copy-start.10 = (f32[1,2,96]{2,1,0:T(2,128)S(1)}, f32[1,2,96]{2,1,0:T(2,128)}, u32[]{:S(2)}) copy-start(f32[1,2,96]{2,1,0:T(2,128)} %param.13) | copy-start | bytes 2308
  45.0 21.0 %copy-start.5 = (s32[2]{0:T(128)S(1)}, s32[2]{0:T(128)}, u32[]{:S(2)}) copy-start(s32[2]{0:T(128)} %copy-done.4) | copy-start | bytes 28
  45.0 21.0 %copy-start.6 = (f32[1,96,96]{2,1,0:T(8,128)S(1)}, f32[1,96,96]{2,1,0:T(8,128)}, u32[]{:S(2)}) copy-start(f32[1,96,96]{2,1,0:T(8,128)} %param.11) | copy-start | bytes 110596
  45.0 14.9 %collective-permute-start.5 = (bf16[2,512,128]{2,1,0:T(8,128)(2,1)S(1)}, bf16[2,512,128]{2,1,0:T(8,128)(2,1)S(1)}, u32[]{:S(2)}, u32[]{:S(2)}) collective-permute-start(bf16[2,512,128]{2,1,0:T(8,128)(2,1)S(1)} %get-tuple-element.31), channel_id=1, source_target_pairs={{0,20},{4,16},{8,28},{12,24},{16,4},{20,0},{24,12},{28,8},{1,21},{... | collective-permute-start | bytes 786440 | tf_op jit(solution)/shard_map/ppermute | solution.py:470
  59.9 31.0 %all-to-all-start.1 = ((bf16[8,2,512,128]{3,2,1,0:T(8,128)(2,1)}), bf16[8,2,512,128]{3,2,1,0:T(8,128)(2,1)}, u32[]{:S(2)}, u32[]{:S(2)}) async-start(bf16[8,2,512,128]{3,2,1,0:T(8,128)(2,1)} %get-tuple-element.32), calls=%async_computation.1 | async-start | bytes 4194304 | tf_op jit(solution)/shard_map/all_to_all | solution.py:462
  64.3 1.8 %collective-permute-start.9 = (bf16[2,512,128]{2,1,0:T(8,128)(2,1)S(1)}, bf16[2,512,128]{2,1,0:T(8,128)(2,1)S(1)}, u32[]{:S(2)}, u32[]{:S(2)}) collective-permute-start(bf16[2,512,128]{2,1,0:T(8,128)(2,1)S(1)} %get-tuple-element.38), channel_id=1, source_target_pairs={{0,4},{4,0},{8,12},{12,8},{16,20},{20,16},{24,28},{28,24},{1,5},{5... | collective-permute-start | bytes 786440 | tf_op jit(solution)/shard_map/ppermute | solution.py:470
  66.0 0.8 copy-start.7
  80.6 29.9 %copy-start.1 = (f32[8,96,1024]{2,1,0:T(8,128)S(1)}, f32[8,96,1024]{2,1,0:T(8,128)}, u32[]{:S(2)}) copy-start(f32[8,96,1024]{2,1,0:T(8,128)} %get-tuple-element.39.particular) | copy-start | bytes 9437188
  80.6 28.8 %collective-permute-start.12 = (f32[2,16,512]{2,1,0:T(8,128)S(1)}, f32[2,16,512]{2,1,0:T(8,128)S(1)}, u32[]{:S(2)}, u32[]{:S(2)}) collective-permute-start(f32[2,16,512]{2,1,0:T(8,128)S(1)} %get-tuple-element.40.rest_0_), channel_id=1, source_target_pairs={{0,3},{1,0},{2,1},{3,2},{4,7},{5,4},{6,5},{7,6},{8,11},{9,8},{10,9... | collective-permute-start | bytes 196616 | tf_op jit(solution)/shard_map/ppermute | solution.py:494
  84.8 25.7 %collective-permute-start.11 = (f32[2,16,512]{2,1,0:T(8,128)S(1)}, f32[2,16,512]{2,1,0:T(8,128)S(1)}, u32[]{:S(2)}, u32[]{:S(2)}) collective-permute-start(f32[2,16,512]{2,1,0:T(8,128)S(1)} %get-tuple-element.40.rest_0_), channel_id=1, source_target_pairs={{0,2},{1,3},{2,0},{3,1},{4,6},{5,7},{6,4},{7,5},{8,10},{9,11},{10,... | collective-permute-start | bytes 196616 | tf_op jit(solution)/shard_map/ppermute | solution.py:494
  84.8 25.7 %collective-permute-start.10 = (f32[2,16,512]{2,1,0:T(8,128)S(1)}, f32[2,16,512]{2,1,0:T(8,128)S(1)}, u32[]{:S(2)}, u32[]{:S(2)}) collective-permute-start(f32[2,16,512]{2,1,0:T(8,128)S(1)} %get-tuple-element.40.rest_0_), channel_id=1, source_target_pairs={{0,1},{1,2},{2,3},{3,0},{4,5},{5,6},{6,7},{7,4},{8,9},{9,10},{10,1... | collective-permute-start | bytes 196616 | tf_op jit(solution)/shard_map/ppermute | solution.py:494
  90.9 0.8 copy-start.8
  91.7 1.6 %copy-start.9 = (bf16[8,128,1024]{2,1,0:T(8,128)(2,1)S(1)}, bf16[8,128,1024]{2,1,0:T(8,128)(2,1)}, u32[]{:S(2)}) copy-start(bf16[8,128,1024]{2,1,0:T(8,128)(2,1)} %constant.17.clone.table_ref) | copy-start | bytes 6291460
  105.3 11.4 %collective-permute-start.8 = (f32[2,16,512]{2,1,0:T(8,128)S(1)}, f32[2,16,512]{2,1,0:T(8,128)S(1)}, u32[]{:S(2)}, u32[]{:S(2)}) collective-permute-start(f32[2,16,512]{2,1,0:T(8,128)S(1)} %get-tuple-element.36.rest_0_), channel_id=1, source_target_pairs={{0,3},{1,0},{2,1},{3,2},{4,7},{5,4},{6,5},{7,6},{8,11},{9,8},{10,9... | collective-permute-start | bytes 196616 | tf_op jit(solution)/shard_map/ppermute | solution.py:494
  109.4 7.2 %collective-permute-start.7 = (f32[2,16,512]{2,1,0:T(8,128)S(1)}, f32[2,16,512]{2,1,0:T(8,128)S(1)}, u32[]{:S(2)}, u32[]{:S(2)}) collective-permute-start(f32[2,16,512]{2,1,0:T(8,128)S(1)} %get-tuple-element.36.rest_0_), channel_id=1, source_target_pairs={{0,2},{1,3},{2,0},{3,1},{4,6},{5,7},{6,4},{7,5},{8,10},{9,11},{10,... | collective-permute-start | bytes 196616 | tf_op jit(solution)/shard_map/ppermute | solution.py:494
  109.5 7.2 %collective-permute-start.6 = (f32[2,16,512]{2,1,0:T(8,128)S(1)}, f32[2,16,512]{2,1,0:T(8,128)S(1)}, u32[]{:S(2)}, u32[]{:S(2)}) collective-permute-start(f32[2,16,512]{2,1,0:T(8,128)S(1)} %get-tuple-element.36.rest_0_), channel_id=1, source_target_pairs={{0,1},{1,2},{2,3},{3,0},{4,5},{5,6},{6,7},{7,4},{8,9},{9,10},{10,1... | collective-permute-start | bytes 196616 | tf_op jit(solution)/shard_map/ppermute | solution.py:494
  110.5 6.2 %copy-start = (f32[8,96,1024]{2,1,0:T(8,128)S(1)}, f32[8,96,1024]{2,1,0:T(8,128)}, u32[]{:S(2)}) copy-start(f32[8,96,1024]{2,1,0:T(8,128)} %get-tuple-element.33.particular) | copy-start | bytes 9437188

commit v3 on v2

--- a/solution.py
+++ b/solution.py
@@ -314,7 +314,7 @@
             pltpu.SemaphoreType.DMA((size + 1,)),
             pltpu.SemaphoreType.DMA((size * CHUNK,)),
         ],
-        compiler_params=params(),
+        compiler_params=params(58 * 1024 * 1024),
         cost_estimate=pl.CostEstimate(flops=2 * flops, bytes_accessed=4 << 20, transcendentals=0),
         name="stream",
     )(where, prev, tables, m_map, v_map, ends, lam, *flat)

time: 123 us -> 123 us (level)
  Pallas kernels: 57.9 us -> 60.6 us
  waiting for transfers between devices: 33.7 us -> 32.2 us
    pallas_call x2, Pallas kernels: 25.7 us -> 28.3 us  [stream_group(): pl.pallas_call(functools.partial(stream_kernel, modes_count, parts, first...]
    ppermute x7, waiting for transfers between devices: 28.6 us -> 26.8 us  [apart_exchange(): got[step] = lax.ppermute(values[step], 'modes', pairs)]
    unnamed x24 -> x38, local copies, waits for them, and re-layouts: 4.17 us -> 3.18 us
  transfers between devices with their start and end apart: 15 -> 15, of which waited for: 5 -> 5; matrix products, arithmetic and copies ran while one was open for 0% -> 1% of each run, Pallas kernels for 37% -> 40%
where the time goes in v3:
time: 123 us
  Pallas kernels  60.6 us (49%)
  waiting for transfers between devices  32.2 us (26%)
  starting transfers between devices  25.5 us (21%)
  local copies, waits for them, and re-layouts  4.49 us (4%)
    pallas_call x2, Pallas kernels, stream_group(): pl.pallas_call(functools.partial(stream_kernel, modes_count, parts, first...  28.3 us
    ppermute x7, waiting for transfers between devices, apart_exchange(): got[step] = lax.ppermute(values[step], 'modes', pairs)  26.8 us
    pallas_call x2, Pallas kernels, span_part(): pl.pallas_call(functools.partial(span_kernel, modes_count, sets, block),...  15 us
    pallas_call x2, Pallas kernels, finish_group(): pl.pallas_call(functools.partial(finish_kernel, first, kz_local, n_sub, h...  12.3 us
    all_to_all x2, starting transfers between devices, joined_exchange(): got = lax.all_to_all(value, 'modes', 0, 0, tiled=True)  9.65 us
    ppermute x6, starting transfers between devices, chunked(): lax.ppermute(traces, 'sub', [(d, (d + shift) % n_sub) for d in range(n_su...  9.33 us
    ppermute x7, starting transfers between devices, apart_exchange(): got[step] = lax.ppermute(values[step], 'modes', pairs)  6.5 us
    all_to_all x2, waiting for transfers between devices, joined_exchange(): got = lax.all_to_all(value, 'modes', 0, 0, tiled=True)  5.38 us
  transfers between devices with their start and end apart: 15, of which 5 were waited for; matrix products, arithmetic and copies ran while one was open for 1% of the time, Pallas kernels for 40%

profile of v3, /device:TPU:0, one launch (start us, length us, event | category | flops | bytes accessed | tf_op | source)
XLA Modules:
  0.0 123.0 jit_solution(4724866869558760845)
XLA Ops:
  0.0 0.1 pad_add_fusion.where
  0.1 0.9 copy-done.2
  1.0 5.8 %span.2 = bf16[8,4,256,128]{3,2,1,0:T(8,128)(2,1)} custom-call(s32[2]{0:T(128)S(1)} %pad_add_fusion.where, bf16[2,96,128,512]{3,2,1,0:T(8,128)(2,1)} %fields.3, bf16[8,32,512]{2,1,0:T(8,128)(2,1)S(1)} %copy-done.2), custom_call_target="tpu_custom_call" | custom-call | flops 1073741824 | bytes 10485760 | tf_op jit(solution)/shard_map/span/pallas_call | solution.py:125
  6.8 5.3 %all-to-all-start = ((bf16[8,4,256,128]{3,2,1,0:T(8,128)(2,1)}), bf16[8,4,256,128]{3,2,1,0:T(8,128)(2,1)S(1)}, u32[]{:S(2)}, u32[]{:S(2)}) async-start(bf16[8,4,256,128]{3,2,1,0:T(8,128)(2,1)} %span.2), calls=%async_computation | async-start | bytes 4194304 | tf_op jit(solution)/shard_map/all_to_all | solution.py:462
  12.1 9.2 %span.3 = (bf16[2,512,128]{2,1,0:T(8,128)(2,1)S(1)}, bf16[2,512,128]{2,1,0:T(8,128)(2,1)S(1)}, bf16[2,512,128]{2,1,0:T(8,128)(2,1)S(1)}, bf16[2,512,128]{2,1,0:T...) custom-call(s32[2]{0:T(128)S(1)} %pad_add_fusion.where, ...), custom_call_target="tpu_custom_call" | custom-call | flops 2147483648 | bytes 20971520 | tf_op jit(solution)/shard_map/span/pallas_call | solution.py:125
  21.3 0.7 copy-done.8
  22.1 2.9 %collective-permute-start = (bf16[2,512,128]{2,1,0:T(8,128)(2,1)S(1)}, bf16[2,512,128]{2,1,0:T(8,128)(2,1)S(1)}, u32[]{:S(2)}, u32[]{:S(2)}) collective-permute-start(bf16[2,512,128]{2,1,0:T(8,128)(2,1)S(1)} %get-tuple-element.26), channel_id=1, source_target_pairs={{0,24},{4,28},{8,16},{12,20},{16,8},{20,12},{24,0},{28,4},{1,25},{... | collective-permute-start | bytes 786440 | tf_op jit(solution)/shard_map/ppermute | solution.py:470
  25.0 1.5 %collective-permute-start.2 = (bf16[2,512,128]{2,1,0:T(8,128)(2,1)S(1)}, bf16[2,512,128]{2,1,0:T(8,128)(2,1)S(1)}, u32[]{:S(2)}, u32[]{:S(2)}) collective-permute-start(bf16[2,512,128]{2,1,0:T(8,128)(2,1)S(1)} %get-tuple-element.28), channel_id=1, source_target_pairs={{0,8},{4,12},{8,0},{12,4},{16,24},{20,28},{24,16},{28,20},{1,9},{5... | collective-permute-start | bytes 786440 | tf_op jit(solution)/shard_map/ppermute | solution.py:470
  26.5 1.5 %collective-permute-start.3 = (bf16[2,512,128]{2,1,0:T(8,128)(2,1)S(1)}, bf16[2,512,128]{2,1,0:T(8,128)(2,1)S(1)}, u32[]{:S(2)}, u32[]{:S(2)}) collective-permute-start(bf16[2,512,128]{2,1,0:T(8,128)(2,1)S(1)} %get-tuple-element.29), channel_id=1, source_target_pairs={{0,16},{4,20},{8,24},{12,28},{16,0},{20,4},{24,8},{28,12},{1,17},{... | collective-permute-start | bytes 786440 | tf_op jit(solution)/shard_map/ppermute | solution.py:470
  28.0 0.2 collective-permute-start.4
  28.2 16.8 %collective-permute-done.rest_7_ = bf16[2,512,128]{2,1,0:T(8,128)(2,1)S(1)} collective-permute-done((bf16[2,512,128]{2,1,0:T(8,128)(2,1)S(1)}, bf16[2,512,128]{2,1,0:T(8,128)(2,1)S(1)}, u32[]{:S(2)}, u32[]{:S(2)}) %collective-permute-start) | collective-permute-done | bytes 262176 | tf_op jit(solution)/shard_map/ppermute | solution.py:470
  45.0 5.0 %wall.1 = (f32[16,96,512]{2,1,0:T(8,128)}, f32[16,96,512]{2,1,0:T(8,128)}) custom-call(s32[2]{0:T(128)} %copy-done.6), custom_call_target="tpu_custom_call" | custom-call | flops 16777216 | bytes 6291456 | tf_op jit(solution)/shard_map/wall/pallas_call | solution.py:339
  50.0 5.3 %collective-permute-done.2.rest_3_ = bf16[2,512,128]{2,1,0:T(8,128)(2,1)S(1)} collective-permute-done((bf16[2,512,128]{2,1,0:T(8,128)(2,1)S(1)}, bf16[2,512,128]{2,1,0:T(8,128)(2,1)S(1)}, u32[]{:S(2)}, u32[]{:S(2)}) %collective-permute-start.2) | collective-permute-done | bytes 262176 | tf_op jit(solution)/shard_map/ppermute | solution.py:470
  55.2 4.7 %collective-permute-done.4.rest_4_ = bf16[2,512,128]{2,1,0:T(8,128)(2,1)S(1)} collective-permute-done((bf16[2,512,128]{2,1,0:T(8,128)(2,1)S(1)}, bf16[2,512,128]{2,1,0:T(8,128)(2,1)S(1)}, u32[]{:S(2)}, u32[]{:S(2)}) %collective-permute-start.4) | collective-permute-done | bytes 262176 | tf_op jit(solution)/shard_map/ppermute | solution.py:470
  59.9 0.7 copy-done.16
  60.6 0.1 copy-done.17
  60.7 4.3 %all-to-all-start.1 = ((bf16[8,2,512,128]{3,2,1,0:T(8,128)(2,1)}), bf16[8,2,512,128]{3,2,1,0:T(8,128)(2,1)}, u32[]{:S(2)}, u32[]{:S(2)}) async-start(bf16[8,2,512,128]{3,2,1,0:T(8,128)(2,1)} %get-tuple-element.32), calls=%async_computation.1 | async-start | bytes 4194304 | tf_op jit(solution)/shard_map/all_to_all | solution.py:462
  65.1 0.4 collective-permute-start.9
  65.4 0.7 copy.11.lam
  66.2 0.6 pad.4.e_ref
  66.7 0.1 collective-permute-done.9.rest_2_
  66.8 0.7 copy-done.18
  67.5 14.1 %stream.3 = (f32[8,96,1024]{2,1,0:T(8,128)}, f32[2,16,512]{2,1,0:T(8,128)}) custom-call(s32[2]{0:T(128)} %copy-done.6, f32[96,128,128]{2,1,0:T(8,128)} %bitcast.18, bf16[8,128,1024]{2,1,0:T(8,128)(2,1)} %constant.17.clone.table_ref, f32[96,96]{1,0:T(8,128)} %bitcast.20, f32[96,96]{1,0:T(8,128)} %bitcast.22, f32[8,96]{1,0:T(8,128)} %pad.4.e_ref, ...), custom_call_target="tpu_custom_call" | custom-call | flops 6442450944 | bytes 4194304 | tf_op jit(solution)/shard_map/stream/pallas_call | solution.py:296
  81.6 0.0 copy-start.1
  81.7 3.6 %collective-permute-start.12 = (f32[2,16,512]{2,1,0:T(8,128)}, f32[2,16,512]{2,1,0:T(8,128)S(1)}, u32[]{:S(2)}, u32[]{:S(2)}) collective-permute-start(f32[2,16,512]{2,1,0:T(8,128)} %get-tuple-element.40.rest_0_), channel_id=1, source_target_pairs={{0,3},{1,0},{2,1},{3,2},{4,7},{5,4},{6,5},{7,6},{8,11},{9,8},{10,9... | collective-permute-start | bytes 196616 | tf_op jit(solution)/shard_map/ppermute | solution.py:494
  85.3 1.0 collective-permute-start.10
  86.3 5.4 %all-to-all-done.1.rest_1_ = bf16[8,2,512,128]{3,2,1,0:T(8,128)(2,1)} async-done(((bf16[8,2,512,128]{3,2,1,0:T(8,128)(2,1)}), bf16[8,2,512,128]{3,2,1,0:T(8,128)(2,1)}, u32[]{:S(2)}, u32[]{:S(2)}) %all-to-all-start.1) | async-done | bytes 2097184 | tf_op jit(solution)/shard_map/all_to_all | solution.py:462
  91.7 14.2 %stream.2 = (f32[8,96,1024]{2,1,0:T(8,128)}, f32[2,16,512]{2,1,0:T(8,128)}) custom-call(s32[2]{0:T(128)} %copy-done.6, f32[96,128,128]{2,1,0:T(8,128)} %bitcast.19, bf16[8,128,1024]{2,1,0:T(8,128)(2,1)} %constant.17.clone.table_ref, f32[96,96]{1,0:T(8,128)} %bitcast.21, f32[96,96]{1,0:T(8,128)} %bitcast.23, f32[8,96]{1,0:T(8,128)} %pad.4.e_ref, ...), custom_call_target="tpu_custom_call" | custom-call | flops 6442450944 | bytes 4194304 | tf_op jit(solution)/shard_map/stream/pallas_call | solution.py:296
  105.9 3.7 %collective-permute-start.8 = (f32[2,16,512]{2,1,0:T(8,128)}, f32[2,16,512]{2,1,0:T(8,128)S(1)}, u32[]{:S(2)}, u32[]{:S(2)}) collective-permute-start(f32[2,16,512]{2,1,0:T(8,128)} %get-tuple-element.36.rest_0_), channel_id=1, source_target_pairs={{0,3},{1,0},{2,1},{3,2},{4,7},{5,4},{6,5},{7,6},{8,11},{9,8},{10,9... | collective-permute-start | bytes 196616 | tf_op jit(solution)/shard_map/ppermute | solution.py:494
  109.6 1.0 collective-permute-start.6
  110.7 6.2 %finish.2.rest_4_ = f32[96,128,128]{2,1,0:T(8,128)} custom-call(s32[2]{0:T(128)S(1)} %copy-done.7, f32[8,96,1024]{2,1,0:T(8,128)S(1)} %copy-done.1, f32[16,96,512]{2,1,0:T(8,128)} %get-tuple-element.34.lower, f32[16,96,512]{2,1,0:T(8,128)} %get-tuple-element.35.upper, f32[2,16,512]{2,1,0:T(8,128)S(1)} %copy-done.4, ...), custom_call_target="tpu_custom_call" | custom-call | flops 4194304 | bytes 4194304 | tf_op jit(solution)/shard_map/finish/pallas_call | solution.py:413
  116.9 6.0 %finish.3 = f32[96,128,128]{2,1,0:T(8,128)} custom-call(s32[2]{0:T(128)S(1)} %copy-done.7, f32[8,96,1024]{2,1,0:T(8,128)S(1)} %copy-done, f32[16,96,512]{2,1,0:T(8,128)} %get-tuple-element.34.lower, f32[16,96,512]{2,1,0:T(8,128)} %get-tuple-element.35.upper, f32[2,16,512]{2,1,0:T(8,128)S(1)} %copy-done.5, ...), custom_call_target="tpu_custom_call", output_to_operand_aliasing={{}: (8, {})} | custom-call | flops 4194304 | bytes 4194304 | tf_op jit(solution)/shard_map/finish/pallas_call | solution.py:413
  (46 shorter events, 0.1 us)
Async XLA Ops:
  0.1 0.9 copy-start.2
  1.0 11.1 %copy-start.6 = (s32[2]{0:T(128)}, s32[2]{0:T(128)S(1)}, u32[]{:S(2)}) copy-start(s32[2]{0:T(128)S(1)} %pad_add_fusion.where) | copy-start | bytes 28
  6.8 5.3 %copy-start.3 = (bf16[8,32,512]{2,1,0:T(8,128)(2,1)S(1)}, bf16[8,32,512]{2,1,0:T(8,128)(2,1)}, u32[]{:S(2)}) copy-start(bf16[8,32,512]{2,1,0:T(8,128)(2,1)} %constant.16.clone.table) | copy-start | bytes 786436
  6.8 53.9 %all-to-all-start = ((bf16[8,4,256,128]{3,2,1,0:T(8,128)(2,1)}), bf16[8,4,256,128]{3,2,1,0:T(8,128)(2,1)S(1)}, u32[]{:S(2)}, u32[]{:S(2)}) async-start(bf16[8,4,256,128]{3,2,1,0:T(8,128)(2,1)} %span.2), calls=%async_computation | async-start | bytes 4194304 | tf_op jit(solution)/shard_map/all_to_all | solution.py:462
  21.3 0.7 copy-start.8
  22.1 22.9 %collective-permute-start = (bf16[2,512,128]{2,1,0:T(8,128)(2,1)S(1)}, bf16[2,512,128]{2,1,0:T(8,128)(2,1)S(1)}, u32[]{:S(2)}, u32[]{:S(2)}) collective-permute-start(bf16[2,512,128]{2,1,0:T(8,128)(2,1)S(1)} %get-tuple-element.26), channel_id=1, source_target_pairs={{0,24},{4,28},{8,16},{12,20},{16,8},{20,12},{24,0},{28,4},{1,25},{... | collective-permute-start | bytes 786440 | tf_op jit(solution)/shard_map/ppermute | solution.py:470
  25.0 25.0 %collective-permute-start.1 = (bf16[2,512,128]{2,1,0:T(8,128)(2,1)S(1)}, bf16[2,512,128]{2,1,0:T(8,128)(2,1)S(1)}, u32[]{:S(2)}, u32[]{:S(2)}) collective-permute-start(bf16[2,512,128]{2,1,0:T(8,128)(2,1)S(1)} %get-tuple-element.27), channel_id=1, source_target_pairs={{0,28},{4,24},{8,20},{12,16},{16,12},{20,8},{24,4},{28,0},{1,29},{... | collective-permute-start | bytes 786440 | tf_op jit(solution)/shard_map/ppermute | solution.py:470
  25.0 30.2 %collective-permute-start.2 = (bf16[2,512,128]{2,1,0:T(8,128)(2,1)S(1)}, bf16[2,512,128]{2,1,0:T(8,128)(2,1)S(1)}, u32[]{:S(2)}, u32[]{:S(2)}) collective-permute-start(bf16[2,512,128]{2,1,0:T(8,128)(2,1)S(1)} %get-tuple-element.28), channel_id=1, source_target_pairs={{0,8},{4,12},{8,0},{12,4},{16,24},{20,28},{24,16},{28,20},{1,9},{5... | collective-permute-start | bytes 786440 | tf_op jit(solution)/shard_map/ppermute | solution.py:470
  26.5 28.8 %collective-permute-start.3 = (bf16[2,512,128]{2,1,0:T(8,128)(2,1)S(1)}, bf16[2,512,128]{2,1,0:T(8,128)(2,1)S(1)}, u32[]{:S(2)}, u32[]{:S(2)}) collective-permute-start(bf16[2,512,128]{2,1,0:T(8,128)(2,1)S(1)} %get-tuple-element.29), channel_id=1, source_target_pairs={{0,16},{4,20},{8,24},{12,28},{16,0},{20,4},{24,8},{28,12},{1,17},{... | collective-permute-start | bytes 786440 | tf_op jit(solution)/shard_map/ppermute | solution.py:470
  28.0 31.9 %collective-permute-start.4 = (bf16[2,512,128]{2,1,0:T(8,128)(2,1)S(1)}, bf16[2,512,128]{2,1,0:T(8,128)(2,1)S(1)}, u32[]{:S(2)}, u32[]{:S(2)}) collective-permute-start(bf16[2,512,128]{2,1,0:T(8,128)(2,1)S(1)} %get-tuple-element.30), channel_id=1, source_target_pairs={{0,12},{4,8},{8,4},{12,0},{16,28},{20,24},{24,20},{28,16},{1,13},{... | collective-permute-start | bytes 786440 | tf_op jit(solution)/shard_map/ppermute | solution.py:470
  45.0 15.7 %copy-start.12 = (bf16[2,512,128]{2,1,0:T(8,128)(2,1)}, bf16[2,512,128]{2,1,0:T(8,128)(2,1)S(1)}, u32[]{:S(2)}) copy-start(bf16[2,512,128]{2,1,0:T(8,128)(2,1)S(1)} %collective-permute-done.rest_7_) | copy-start | bytes 786436
  45.0 20.5 %copy-start.11 = (f32[96]{0:T(128)S(1)}, f32[96]{0:T(128)}, u32[]{:S(2)}) copy-start(f32[96]{0:T(128)} %param.12) | copy-start | bytes 1156
  45.0 21.2 %copy-start.10 = (f32[1,2,96]{2,1,0:T(2,128)S(1)}, f32[1,2,96]{2,1,0:T(2,128)}, u32[]{:S(2)}) copy-start(f32[1,2,96]{2,1,0:T(2,128)} %param.13) | copy-start | bytes 2308
  45.0 14.9 %collective-permute-start.5 = (bf16[2,512,128]{2,1,0:T(8,128)(2,1)S(1)}, bf16[2,512,128]{2,1,0:T(8,128)(2,1)S(1)}, u32[]{:S(2)}, u32[]{:S(2)}) collective-permute-start(bf16[2,512,128]{2,1,0:T(8,128)(2,1)S(1)} %get-tuple-element.31), channel_id=1, source_target_pairs={{0,20},{4,16},{8,28},{12,24},{16,4},{20,0},{24,12},{28,8},{1,21},{... | collective-permute-start | bytes 786440 | tf_op jit(solution)/shard_map/ppermute | solution.py:470
  50.0 16.9 %copy-start.13 = (bf16[2,512,128]{2,1,0:T(8,128)(2,1)}, bf16[2,512,128]{2,1,0:T(8,128)(2,1)S(1)}, u32[]{:S(2)}) copy-start(bf16[2,512,128]{2,1,0:T(8,128)(2,1)S(1)} %collective-permute-done.1.rest_8_) | copy-start | bytes 786436
  55.2 11.6 %copy-start.14 = (bf16[2,512,128]{2,1,0:T(8,128)(2,1)}, bf16[2,512,128]{2,1,0:T(8,128)(2,1)S(1)}, u32[]{:S(2)}) copy-start(bf16[2,512,128]{2,1,0:T(8,128)(2,1)S(1)} %collective-permute-done.2.rest_3_) | copy-start | bytes 786436
  55.2 11.6 %copy-start.15 = (bf16[2,512,128]{2,1,0:T(8,128)(2,1)}, bf16[2,512,128]{2,1,0:T(8,128)(2,1)S(1)}, u32[]{:S(2)}) copy-start(bf16[2,512,128]{2,1,0:T(8,128)(2,1)S(1)} %collective-permute-done.3.rest_5_) | copy-start | bytes 786436
  59.9 0.8 copy-start.17
  60.7 6.1 %copy-start.9 = (bf16[8,4,256,128]{3,2,1,0:T(8,128)(2,1)}, bf16[8,4,256,128]{3,2,1,0:T(8,128)(2,1)S(1)}, u32[]{:S(2)}) copy-start(bf16[8,4,256,128]{3,2,1,0:T(8,128)(2,1)S(1)} %all-to-all-done.rest_0_) | copy-start | bytes 6291460
  60.7 31.0 %all-to-all-start.1 = ((bf16[8,2,512,128]{3,2,1,0:T(8,128)(2,1)}), bf16[8,2,512,128]{3,2,1,0:T(8,128)(2,1)}, u32[]{:S(2)}, u32[]{:S(2)}) async-start(bf16[8,2,512,128]{3,2,1,0:T(8,128)(2,1)} %get-tuple-element.32), calls=%async_computation.1 | async-start | bytes 4194304 | tf_op jit(solution)/shard_map/all_to_all | solution.py:462
  65.1 1.8 %collective-permute-start.9 = (bf16[2,512,128]{2,1,0:T(8,128)(2,1)S(1)}, bf16[2,512,128]{2,1,0:T(8,128)(2,1)S(1)}, u32[]{:S(2)}, u32[]{:S(2)}) collective-permute-start(bf16[2,512,128]{2,1,0:T(8,128)(2,1)S(1)} %get-tuple-element.38), channel_id=1, source_target_pairs={{0,4},{4,0},{8,12},{12,8},{16,20},{20,16},{24,28},{28,24},{1,5},{5... | collective-permute-start | bytes 786440 | tf_op jit(solution)/shard_map/ppermute | solution.py:470
  81.6 29.0 %copy-start.1 = (f32[8,96,1024]{2,1,0:T(8,128)S(1)}, f32[8,96,1024]{2,1,0:T(8,128)}, u32[]{:S(2)}) copy-start(f32[8,96,1024]{2,1,0:T(8,128)} %get-tuple-element.39.particular) | copy-start | bytes 9437188
  81.6 29.0 %copy-start.4 = (f32[2,16,512]{2,1,0:T(8,128)S(1)}, f32[2,16,512]{2,1,0:T(8,128)}, u32[]{:S(2)}) copy-start(f32[2,16,512]{2,1,0:T(8,128)} %get-tuple-element.40.rest_0_) | copy-start | bytes 196612
  81.7 29.0 %copy-start.7 = (s32[2]{0:T(128)S(1)}, s32[2]{0:T(128)}, u32[]{:S(2)}) copy-start(s32[2]{0:T(128)} %copy-done.6) | copy-start | bytes 28
  81.7 27.9 %collective-permute-start.12 = (f32[2,16,512]{2,1,0:T(8,128)}, f32[2,16,512]{2,1,0:T(8,128)S(1)}, u32[]{:S(2)}, u32[]{:S(2)}) collective-permute-start(f32[2,16,512]{2,1,0:T(8,128)} %get-tuple-element.40.rest_0_), channel_id=1, source_target_pairs={{0,3},{1,0},{2,1},{3,2},{4,7},{5,4},{6,5},{7,6},{8,11},{9,8},{10,9... | collective-permute-start | bytes 196616 | tf_op jit(solution)/shard_map/ppermute | solution.py:494
  85.3 25.3 %collective-permute-start.11 = (f32[2,16,512]{2,1,0:T(8,128)}, f32[2,16,512]{2,1,0:T(8,128)S(1)}, u32[]{:S(2)}, u32[]{:S(2)}) collective-permute-start(f32[2,16,512]{2,1,0:T(8,128)} %get-tuple-element.40.rest_0_), channel_id=1, source_target_pairs={{0,2},{1,3},{2,0},{3,1},{4,6},{5,7},{6,4},{7,5},{8,10},{9,11},{10,... | collective-permute-start | bytes 196616 | tf_op jit(solution)/shard_map/ppermute | solution.py:494
  85.3 25.3 %collective-permute-start.10 = (f32[2,16,512]{2,1,0:T(8,128)}, f32[2,16,512]{2,1,0:T(8,128)S(1)}, u32[]{:S(2)}, u32[]{:S(2)}) collective-permute-start(f32[2,16,512]{2,1,0:T(8,128)} %get-tuple-element.40.rest_0_), channel_id=1, source_target_pairs={{0,1},{1,2},{2,3},{3,0},{4,5},{5,6},{6,7},{7,4},{8,9},{9,10},{10,1... | collective-permute-start | bytes 196616 | tf_op jit(solution)/shard_map/ppermute | solution.py:494
  105.9 11.0 %collective-permute-start.8 = (f32[2,16,512]{2,1,0:T(8,128)}, f32[2,16,512]{2,1,0:T(8,128)S(1)}, u32[]{:S(2)}, u32[]{:S(2)}) collective-permute-start(f32[2,16,512]{2,1,0:T(8,128)} %get-tuple-element.36.rest_0_), channel_id=1, source_target_pairs={{0,3},{1,0},{2,1},{3,2},{4,7},{5,4},{6,5},{7,6},{8,11},{9,8},{10,9... | collective-permute-start | bytes 196616 | tf_op jit(solution)/shard_map/ppermute | solution.py:494
  109.6 7.3 %collective-permute-start.7 = (f32[2,16,512]{2,1,0:T(8,128)}, f32[2,16,512]{2,1,0:T(8,128)S(1)}, u32[]{:S(2)}, u32[]{:S(2)}) collective-permute-start(f32[2,16,512]{2,1,0:T(8,128)} %get-tuple-element.36.rest_0_), channel_id=1, source_target_pairs={{0,2},{1,3},{2,0},{3,1},{4,6},{5,7},{6,4},{7,5},{8,10},{9,11},{10,... | collective-permute-start | bytes 196616 | tf_op jit(solution)/shard_map/ppermute | solution.py:494
  109.6 7.3 %collective-permute-start.6 = (f32[2,16,512]{2,1,0:T(8,128)}, f32[2,16,512]{2,1,0:T(8,128)S(1)}, u32[]{:S(2)}, u32[]{:S(2)}) collective-permute-start(f32[2,16,512]{2,1,0:T(8,128)} %get-tuple-element.36.rest_0_), channel_id=1, source_target_pairs={{0,1},{1,2},{2,3},{3,0},{4,5},{5,6},{6,7},{7,4},{8,9},{9,10},{10,1... | collective-permute-start | bytes 196616 | tf_op jit(solution)/shard_map/ppermute | solution.py:494
  110.6 6.3 %copy-start = (f32[8,96,1024]{2,1,0:T(8,128)S(1)}, f32[8,96,1024]{2,1,0:T(8,128)}, u32[]{:S(2)}) copy-start(f32[8,96,1024]{2,1,0:T(8,128)} %get-tuple-element.33.particular) | copy-start | bytes 9437188
  110.6 6.3 %copy-start.5 = (f32[2,16,512]{2,1,0:T(8,128)S(1)}, f32[2,16,512]{2,1,0:T(8,128)}, u32[]{:S(2)}) copy-start(f32[2,16,512]{2,1,0:T(8,128)} %get-tuple-element.36.rest_0_) | copy-start | bytes 196612
  (2 other events, 1.4 us)
